TPU v7x, 512 devices: a whole 4x8x8 slice. The times are simulated.
512 devices in a mesh: dp: 64 (over z_hi, y, core), group: 8 (over x, z_lo).
Axes of the slice: x: 4, y: 8, z: 8 (z_hi: 4, z_lo: 2; z = z_hi * 2 + z_lo), core: 2. Of those that a mesh axis runs over, the one named last changes fastest.
Arguments:
- tokens: bfloat16 [49152, 1024], P('dp'), may hold values from -100 to 100
- cotangent: bfloat16 [49152, 8192], P('dp', 'group'), may hold values from -3 to 3
Outputs:
- update: bfloat16 [1024, 8192], P('dp', 'group')
All inputs are finite; a program needn't handle non-finite values.
Results may differ from a plain program's by a relative error of at most 0.0025.
The roundings to bfloat16 on the way count: a program that leaves them out, or rounds other values in their place, can miss the bound.
Values may be sent and summed in bfloat16 or wider, within the bound.
No kernel may reach another device: no remote copies, remote signals or barrier semaphores. Data moves between devices by JAX's collectives and lax.ppermute only.
A program may use at most 64 MiB of HBM per device.

v0:
```python
import jax
import jax.numpy as jnp
from jax import lax
from jax.sharding import PartitionSpec as P

ITERS = 2


def on_device(tokens, cotangent):
    width = tokens.shape[1]
    slab_rows = width // lax.axis_size("dp")
    first_row = lax.axis_index("dp") * slab_rows
    identity = jnp.eye(width, dtype=jnp.float32)
    gradient_rows = lax.psum_scatter(
        lax.dot_general(
            tokens, cotangent, (((0,), (0,)), ((), ())), preferred_element_type=jnp.float32
        ),
        "dp",
        scatter_dimension=0,
        tiled=True,
    )
    gradient_b = gradient_rows.astype(jnp.bfloat16)
    gradient_full = lax.all_gather(gradient_b, "dp", axis=0, tiled=True)
    own_columns = lax.dynamic_slice_in_dim(gradient_full, first_row, slab_rows, 1)
    left_rows = lax.dot_general(
        gradient_b, gradient_full, (((1,), (1,)), ((), ())), preferred_element_type=jnp.float32
    )
    right_rows = lax.dot_general(
        own_columns, gradient_full, (((0,), (0,)), ((), ())), preferred_element_type=jnp.float32
    )
    left_square, right_square = lax.psum(
        (jnp.sum(left_rows * left_rows), jnp.sum(right_rows * right_rows)), "dp"
    )
    left_slab = (left_rows / jnp.sqrt(left_square)).astype(jnp.bfloat16)
    right_slab = (right_rows / jnp.sqrt(right_square)).astype(jnp.bfloat16)
    left_full, right_full = (
        lax.all_gather(left_slab, "dp", axis=0, tiled=True),
        lax.all_gather(right_slab, "dp", axis=0, tiled=True),
    )
    right_factors = []
    left_root = left_slab
    for step in range(ITERS):
        if step > 0:
            left_full, right_full = (
                lax.all_gather(left_slab, "dp", axis=0, tiled=True),
                lax.all_gather(right_slab, "dp", axis=0, tiled=True),
            )
        left_factor = ((5.0 * identity - left_full.astype(jnp.float32)) / 4.0).astype(jnp.bfloat16)
        right_factor = ((5.0 * identity - right_full.astype(jnp.float32)) / 4.0).astype(
            jnp.bfloat16
        )
        right_factors.append(right_factor)
        if step < ITERS - 1:
            for power in range(4):
                left_slab = jnp.dot(
                    left_slab, left_factor, preferred_element_type=jnp.float32
                ).astype(jnp.bfloat16)
                right_slab = jnp.dot(
                    right_slab, right_factor, preferred_element_type=jnp.float32
                ).astype(jnp.bfloat16)
        if step == 0:
            left_root = lax.dynamic_slice_in_dim(left_factor, first_row, slab_rows, 0)
        else:
            left_root = jnp.dot(left_root, left_factor, preferred_element_type=jnp.float32).astype(
                jnp.bfloat16
            )
    chain = jnp.dot(left_root, gradient_full, preferred_element_type=jnp.float32).astype(
        jnp.bfloat16
    )
    step = 0
    chain = jnp.dot(chain, right_factors[step], preferred_element_type=jnp.float32).astype(
        jnp.bfloat16
    )
    precond = jnp.dot(chain, right_factors[ITERS - 1], preferred_element_type=jnp.float32)
    square_sum = lax.psum(jnp.sum(precond * precond), ("dp", "group"))
    mean_square = square_sum / (lax.axis_size("group") * width * width)
    return (precond / jnp.sqrt(mean_square + 1e-06)).astype(jnp.bfloat16)


def solution(mesh):
    return jax.shard_map(
        on_device,
        mesh=mesh,
        in_specs=(P("dp", None), P("dp", "group")),
        out_specs=P("dp", "group"),
        check_vma=False,
    )
```

profile of v0, /device:TPU:1, one launch (start us, length us, event | category | flops | bytes accessed | tf_op | source)
XLA Modules:
  0.0 853.2 jit_solution(15196379752362576442)
XLA Ops:
  6.5 0.0 copy-start
  6.5 0.0 reduce-scatter.2.cloned.1.call-start
  6.5 1.4 copy-done
  7.9 5.2 fusion.50
  13.1 0.0 reduce-scatter.2.cloned.1.call-update
  13.2 0.0 all-gather.6.cloned.1.call-start
  13.2 158.0 %reduce-scatter.2.cloned.1.call-done = f32[16,1024]{1,0:T(8,128)} async-done(((f32[1024,1024]{1,0:T(8,128)}), f32[16,1024]{1,0:T(8,128)}) %reduce-scatter.2.cloned.1.call-update) | async-done | bytes 65552 | tf_op jit(solution)/shard_map/reduce_scatter | solution.py:14
  171.2 1.5 convert_element_type.70
  172.7 0.0 all-gather.6.cloned.1.call-update
  172.7 0.0 all-gather.8.cloned.1.call-start
  172.7 88.9 %all-gather.6.cloned.1.call-done = bf16[1024,1024]{1,0:T(8,128)(2,1)} async-done(((bf16[16,1024]{1,0:T(8,128)(2,1)}), bf16[1024,1024]{1,0:T(8,128)(2,1)}) %all-gather.6.cloned.1.call-update) | async-done | bytes 2097168 | tf_op jit(solution)/shard_map/all_gather | solution.py:23
  261.6 2.9 multiply_reduce_fusion.2
  264.6 2.9 multiply_reduce_fusion.1
  267.4 138.7 %all-reduce = (f32[]{:T(128)}, f32[]{:T(128)}) all-reduce(f32[]{:T(128)} %get-tuple-element.7, f32[]{:T(128)} %get-tuple-element.9), channel_id=1, replica_groups=mesh['dp'=64,'group'=8] {'dp'}, use_global_device_ids=true, to_apply=%region_2.0 | all-reduce | flops 2 | bytes 16 | tf_op jit(solution)/shard_map/psum | solution.py:31
  406.8 0.6 divide_convert_fusion.2
  407.5 0.0 all-gather.8.cloned.1.call-update
  407.5 0.0 all-gather.12.cloned.1.call-start
  408.3 0.6 divide_convert_fusion.1
  408.9 0.0 all-gather.12.cloned.1.call-update
  408.9 0.0 all-gather.10.cloned.1.call-start
  409.0 81.2 %all-gather.8.cloned.1.call-done = bf16[1024,1024]{1,0:T(8,128)(2,1)} async-done(((bf16[16,1024]{1,0:T(8,128)(2,1)}), bf16[1024,1024]{1,0:T(8,128)(2,1)}) %all-gather.8.cloned.1.call-update) | async-done | bytes 2097168 | tf_op jit(solution)/shard_map/all_gather | solution.py:37
  490.2 3.4 convolution_convert_fusion.8
  493.6 0.0 copy-start.1
  493.6 4.0 convolution_convert_fusion.6
  497.6 0.0 all-gather.10.cloned.1.call-update
  497.6 0.0 all-gather.14.cloned.1.call-start
  497.6 78.0 %all-gather.12.cloned.1.call-done = bf16[1024,1024]{1,0:T(8,128)(2,1)} async-done(((bf16[16,1024]{1,0:T(8,128)(2,1)}), bf16[1024,1024]{1,0:T(8,128)(2,1)}) %all-gather.12.cloned.1.call-update) | async-done | bytes 2097168 | tf_op jit(solution)/shard_map/all_gather | solution.py:38
  575.6 0.0 copy-done.1
  575.6 3.3 convolution_convert_fusion.2
  579.0 4.0 convolution_convert_fusion
  582.9 0.0 all-gather.14.cloned.1.call-update
  583.0 3.5 fusion.1
  586.4 74.5 %all-gather.10.cloned.1.call-done = bf16[1024,1024]{1,0:T(8,128)(2,1)} async-done(((bf16[16,1024]{1,0:T(8,128)(2,1)}), bf16[1024,1024]{1,0:T(8,128)(2,1)}) %all-gather.10.cloned.1.call-update) | async-done | bytes 2097168 | tf_op jit(solution)/shard_map/all_gather | solution.py:45
  661.0 2.3 fusion.12
  663.2 3.1 convolution_convert_fusion.4
  666.4 80.0 %all-gather.14.cloned.1.call-done = bf16[1024,1024]{1,0:T(8,128)(2,1)} async-done(((bf16[16,1024]{1,0:T(8,128)(2,1)}), bf16[1024,1024]{1,0:T(8,128)(2,1)}) %all-gather.14.cloned.1.call-update) | async-done | bytes 2097168 | tf_op jit(solution)/shard_map/all_gather | solution.py:46
  746.4 2.8 multiply_reduce_fusion
  749.2 95.8 %psum.23 = f32[]{:T(128)} all-reduce(f32[]{:T(128)} %get-tuple-element.11), channel_id=1, replica_groups=mesh['dp'=64,'group'=8] {'dp','group'}, use_global_device_ids=true, to_apply=%region_6.0 | all-reduce | flops 1 | bytes 8 | tf_op jit(solution)/shard_map/psum | solution.py:75
  845.8 0.6 divide_convert_fusion
Async XLA Ops:
  6.5 1.4 copy-start
  6.5 164.7 %reduce-scatter.2.cloned.1.call-start = ((), (), s32[]{:S(2)}) async-start(), calls=%async_computation.1 | async-start | bytes 4259840 | tf_op jit(solution)/shard_map/reduce_scatter | solution.py:14
  13.2 248.5 %all-gather.6.cloned.1.call-start = ((), (), s32[]{:S(2)}) async-start(), calls=%async_computation.2 | async-start | bytes 2129920 | tf_op jit(solution)/shard_map/all_gather | solution.py:23
  172.7 317.5 %all-gather.8.cloned.1.call-start = ((), (), s32[]{:S(2)}) async-start(), calls=%async_computation.3 | async-start | bytes 2129920 | tf_op jit(solution)/shard_map/all_gather | solution.py:37
  407.5 168.1 %all-gather.12.cloned.1.call-start = ((), (), s32[]{:S(2)}) async-start(), calls=%async_computation.5 | async-start | bytes 2129920 | tf_op jit(solution)/shard_map/all_gather | solution.py:38
  408.9 252.1 %all-gather.10.cloned.1.call-start = ((), (), s32[]{:S(2)}) async-start(), calls=%async_computation.4 | async-start | bytes 2129920 | tf_op jit(solution)/shard_map/all_gather | solution.py:45
  493.6 82.0 %copy-start.1 = (bf16[16,1024]{1,0:T(8,128)(2,1)S(1)}, bf16[16,1024]{1,0:T(8,128)(2,1)}, u32[]{:S(2)}) copy-start(bf16[16,1024]{1,0:T(8,128)(2,1)} %divide_convert_fusion.1) | copy-start | bytes 98308
  497.6 248.8 %all-gather.14.cloned.1.call-start = ((), (), s32[]{:S(2)}) async-start(), calls=%async_computation.6 | async-start | bytes 2129920 | tf_op jit(solution)/shard_map/all_gather | solution.py:46
Sparse Core Ops, SparseCore 0:
  13.3 157.8 reduce-scatter.1
  175.1 86.4 all-gather.5
  407.6 82.5 all-gather.7
  494.0 81.6 all-gather.11
  579.3 81.6 all-gather.9
  664.7 81.6 all-gather.13
where the time goes:
time: 854 us; the launch traced here: 853 us
  waiting for transfers between devices  561 us (66%)
  blocking collectives  235 us (28%)
  matrix products  33.9 us (4%)
  between operations  15.6 us (2%)
    reduce_scatter x1, waiting for transfers between devices, on_device(): lax.psum_scatter(lax.dot_general(tokens, cotangent, (((0,), (0,)), ((), (...  158 us
    all_gather x2, waiting for transfers between devices, on_device(): lax.all_gather(right_slab, 'dp', axis=0, tiled=True)  158 us
    all_gather x2, waiting for transfers between devices, on_device(): lax.all_gather(left_slab, 'dp', axis=0, tiled=True)  156 us
    psum x1, blocking collectives, on_device(): lax.psum((jnp.sum(left_rows * left_rows), jnp.sum(right_rows * right_rows...  139 us
    psum x1, blocking collectives, on_device(): square_sum = lax.psum(jnp.sum(precond * precond), ('dp', 'group'))  95.8 us
    all_gather x1, waiting for transfers between devices, on_device(): gradient_full = lax.all_gather(gradient_b, 'dp', axis=0, tiled=True)  88.9 us
  transfers between devices with their start and end apart: 6, of which 6 were waited for; matrix products, arithmetic and copies ran while one was open for 3% of the time, Pallas kernels for 0%

commit v1 on v0

v1 whole, which is shorter than its diff:
```python
import jax
import jax.numpy as jnp
from jax import lax
from jax.sharding import PartitionSpec as P

ITERS = 2
Z, Y, C = 4, 8, 2


def dp_perm(dz, dy, dc):
    pairs = []
    for z in range(Z):
        for y in range(Y):
            for c in range(C):
                target = ((z + dz) % Z) * Y * C + ((y + dy) % Y) * C + (c + dc) % C
                pairs.append((z * Y * C + y * C + c, target))
    return pairs


def newton(stat, identity):
    iterate = lax.reduce_precision(stat / jnp.sqrt(jnp.sum(stat * stat)), 8, 7)
    factors = []
    for step in range(ITERS):
        factor = ((5.0 * identity - iterate) / 4.0).astype(jnp.bfloat16)
        factors.append(factor)
        if step < ITERS - 1:
            for power in range(4):
                iterate = lax.reduce_precision(
                    jnp.dot(
                        iterate.astype(jnp.bfloat16), factor, preferred_element_type=jnp.float32
                    ),
                    8,
                    7,
                )
    return factors


def on_device(tokens, cotangent):
    width = tokens.shape[1]
    dp = lax.axis_index("dp")
    z, y, c = dp // (Y * C), (dp // C) % Y, dp % C
    identity = jnp.eye(width, dtype=jnp.float32)
    half = width // C
    slab = half // Y
    part = slab // Z

    partial = lax.dot_general(
        tokens, cotangent, (((0,), (0,)), ((), ())), preferred_element_type=jnp.float32
    )
    away = lax.dynamic_slice_in_dim(partial, (1 - c) * half, half, 0)
    near = lax.dynamic_slice_in_dim(partial, c * half, half, 0)
    near = near + lax.ppermute(away, "dp", dp_perm(0, 0, 1))
    got = []
    for k in range(1, Y):
        piece = lax.dynamic_slice_in_dim(near, ((y + k) % Y) * slab, slab, 0)
        got.append(lax.ppermute(piece, "dp", dp_perm(0, k, 0)))
    own = lax.dynamic_slice_in_dim(near, y * slab, slab, 0)
    for piece in got:
        own = own + piece
    got = []
    for k in range(1, Z):
        piece = lax.dynamic_slice_in_dim(own, ((z + k) % Z) * part, part, 0)
        got.append(lax.ppermute(piece, "dp", dp_perm(k, 0, 0)))
    rows = lax.dynamic_slice_in_dim(own, z * part, part, 0)
    for piece in got:
        rows = rows + piece
    rows = rows.astype(jnp.bfloat16)

    def gather(block, size, me, perm_of):
        pieces = [block] + [lax.ppermute(block, "dp", perm_of(size - k)) for k in range(1, size)]
        order = jnp.stack(pieces)
        twice = jnp.concatenate([order, order])
        whole = lax.dynamic_slice_in_dim(twice, (size - me) % size, size, 0)
        return whole.reshape(size * block.shape[0], block.shape[1])

    rows = gather(rows, Z, z, lambda k: dp_perm(k, 0, 0))
    rows = gather(rows, Y, y, lambda k: dp_perm(0, k, 0))
    gradient = gather(rows, C, c, lambda k: dp_perm(0, 0, k))

    left_stat = lax.dot_general(
        gradient, gradient, (((1,), (1,)), ((), ())), preferred_element_type=jnp.float32
    )
    right_stat = lax.dot_general(
        gradient, gradient, (((0,), (0,)), ((), ())), preferred_element_type=jnp.float32
    )
    left = newton(left_stat, identity)
    right = newton(right_stat, identity)
    chain = left[0]
    for factor in left[1:]:
        chain = jnp.dot(chain, factor, preferred_element_type=jnp.float32).astype(jnp.bfloat16)
    chain = jnp.dot(chain, gradient, preferred_element_type=jnp.float32).astype(jnp.bfloat16)
    for factor in right[:-1]:
        chain = jnp.dot(chain, factor, preferred_element_type=jnp.float32).astype(jnp.bfloat16)
    precond = jnp.dot(chain, right[-1], preferred_element_type=jnp.float32)
    square = jnp.broadcast_to(jnp.sum(precond * precond), (8, 128))
    groups = lax.axis_size("group")
    total = square
    for k in range(1, groups):
        total = total + lax.ppermute(square, "group", [(g, (g + k) % groups) for g in range(groups)])
    mean_square = total[0, 0] / (groups * width * width)
    mine = lax.dynamic_slice_in_dim(precond, dp * part, part, 0)
    return (mine / jnp.sqrt(mean_square + 1e-06)).astype(jnp.bfloat16)


def solution(mesh):
    return jax.shard_map(
        on_device,
        mesh=mesh,
        in_specs=(P("dp", None), P("dp", "group")),
        out_specs=P("dp", "group"),
        check_vma=False,
    )
```

time: 854 us -> 289 us (0.34)
  waiting for transfers between devices: 561 us -> 57 us
  blocking collectives: 235 us -> 0 us
  starting transfers between devices: 0.21 us -> 127 us
  matrix products: 33.9 us -> 78.1 us
  between operations: 15.6 us -> 3 us
    all_gather x5 -> x0, waiting for transfers between devices: 403 us -> none  [the longest x2 158 us: on_device(): lax.all_gather(right_slab, 'dp', axis=0, tiled=True)]
    psum x2 -> x0, blocking collectives: 235 us -> none  [the longest x1 139 us: on_device(): lax.psum((jnp.sum(left_rows * left_rows), jnp.sum(right_rows * right_rows...]
    reduce_scatter x1 -> x0, waiting for transfers between devices: 158 us -> none  [on_device(): lax.psum_scatter(lax.dot_general(tokens, cotangent, (((0,), (0,)), ((), (...]
    ppermute x0 -> x29, starting transfers between devices: none -> 127 us  [the longest x11 54.4 us: gather(): lax.ppermute(block, 'dp', perm_of(size - k))]
    ppermute x0 -> x29, waiting for transfers between devices: none -> 57 us  [the longest x7 30.2 us: on_device(): got.append(lax.ppermute(piece, 'dp', dp_perm(0, k, 0)))]
    dot_general x9, matrix products: 28.7 us -> 74.8 us  [the longest x4 34.7 us: newton(): jnp.dot(iterate.astype(jnp.bfloat16), factor, preferred_element_type=jnp....]
  transfers between devices with their start and end apart: 6 -> 29, of which waited for: 6 -> 11; matrix products, arithmetic and copies ran while one was open for 3% -> 0% of each run, Pallas kernels for 0% -> 0%
where the time goes in v1:
time: 289 us; the launch traced here: 283 us
  starting transfers between devices  127 us (44%)
  matrix products  78.1 us (27%)
  waiting for transfers between devices  57 us (20%)
  other arithmetic  8.95 us (3%)
  local copies, waits for them, and re-layouts  8.76 us (3%)
  between operations  3 us (1%)
    ppermute x11, starting transfers between devices, gather(): lax.ppermute(block, 'dp', perm_of(size - k))  54.4 us
    dot_general x4, matrix products, newton(): jnp.dot(iterate.astype(jnp.bfloat16), factor, preferred_element_type=jnp....  34.7 us
    ppermute x7, waiting for transfers between devices, on_device(): got.append(lax.ppermute(piece, 'dp', dp_perm(0, k, 0)))  30.2 us
    ppermute x7, starting transfers between devices, on_device(): lax.ppermute(square, 'group', [(g, (g + k) % groups) for g in range(group...  27 us
    ppermute x7, starting transfers between devices, on_device(): got.append(lax.ppermute(piece, 'dp', dp_perm(0, k, 0)))  23 us
    dot_general x2, matrix products, on_device(): jnp.dot(chain, factor, preferred_element_type=jnp.float32)  19.5 us
    ppermute x11, waiting for transfers between devices, gather(): lax.ppermute(block, 'dp', perm_of(size - k))  15 us
    ppermute x3, starting transfers between devices, on_device(): got.append(lax.ppermute(piece, 'dp', dp_perm(k, 0, 0)))  14 us
  transfers between devices with their start and end apart: 29, of which 11 were waited for; matrix products, arithmetic and copies ran while one was open for 0% of the time, Pallas kernels for 0%

profile of v1, /device:TPU:1, one launch (start us, length us, event | category | flops | bytes accessed | tf_op | source)
XLA Modules:
  0.0 283.1 jit_solution(680670069511204889)
XLA Ops:
  0.0 1.4 copy-done
  1.4 3.2 %fusion.50 = f32[1024,1024]{1,0:T(8,128)S(1)} fusion(bf16[768,1024]{1,0:T(8,128)(2,1)S(1)} %copy-done, bf16[768,1024]{1,0:T(8,128)(2,1)} %param.3), kind=kOutput, calls=%fused_computation.90 | convolution fusion | flops 1610612736 | bytes 7340032 | tf_op jit(solution)/shard_map/dot_general | solution.py:47
  4.7 1.9 copy-done.2
  6.6 1.5 constant_dynamic-slice_fusion.12
  8.2 8.8 %collective-permute-start = (f32[512,1024]{1,0:T(8,128)}, f32[512,1024]{1,0:T(8,128)}, u32[]{:S(2)}, u32[]{:S(2)}) collective-permute-start(f32[512,1024]{1,0:T(8,128)} %constant_dynamic-slice_fusion.12), channel_id=1, source_target_pairs={{0,8},{8,0},{16,24},{24,16},{32,40},{40,32},{48,56},{56,48},{64,72... | collective-permute-start | bytes 6291464 | tf_op jit(solution)/shard_map/ppermute | solution.py:52
  17.1 3.9 %collective-permute-done = f32[512,1024]{1,0:T(8,128)} collective-permute-done((f32[512,1024]{1,0:T(8,128)}, f32[512,1024]{1,0:T(8,128)}, u32[]{:S(2)}, u32[]{:S(2)}) %collective-permute-start) | collective-permute-done | bytes 2097184 | tf_op jit(solution)/shard_map/ppermute | solution.py:52
  21.0 2.6 dynamic-slice_add_fusion
  23.7 1.3 copy-done.1
  25.0 1.0 constant_dynamic-slice_fusion.11
  26.1 1.9 collective-permute-start.1
  28.0 4.6 %collective-permute-start.7 = (f32[64,1024]{1,0:T(8,128)S(1)}, f32[64,1024]{1,0:T(8,128)S(1)}, u32[]{:S(2)}, u32[]{:S(2)}) collective-permute-start(f32[64,1024]{1,0:T(8,128)S(1)} %get-tuple-element.8), channel_id=1, source_target_pairs={{0,112},{8,120},{16,0},{24,8},{32,16},{40,24},{48,32},{56,40},{64,... | collective-permute-start | bytes 786440 | tf_op jit(solution)/shard_map/ppermute | solution.py:56
  32.6 1.9 collective-permute-start.6
  34.5 2.1 collective-permute-start.5
  36.6 7.1 %collective-permute-start.4 = (f32[64,1024]{1,0:T(8,128)}, f32[64,1024]{1,0:T(8,128)S(1)}, u32[]{:S(2)}, u32[]{:S(2)}) collective-permute-start(f32[64,1024]{1,0:T(8,128)} %get-tuple-element.11), channel_id=1, source_target_pairs={{0,64},{8,72},{16,80},{24,88},{32,96},{40,104},{48,112},{56,120},{... | collective-permute-start | bytes 786440 | tf_op jit(solution)/shard_map/ppermute | solution.py:56
  43.7 0.0 collective-permute-done.1
  43.7 1.9 collective-permute-start.3
  45.6 3.5 %collective-permute-start.2 = (f32[64,1024]{1,0:T(8,128)S(1)}, f32[64,1024]{1,0:T(8,128)}, u32[]{:S(2)}, u32[]{:S(2)}) collective-permute-start(f32[64,1024]{1,0:T(8,128)S(1)} %get-tuple-element.13), channel_id=1, source_target_pairs={{0,32},{8,40},{16,48},{24,56},{32,64},{40,72},{48,80},{56,88},{64,... | collective-permute-start | bytes 786440 | tf_op jit(solution)/shard_map/ppermute | solution.py:56
  49.3 1.3 collective-permute-done.6
  50.6 11.4 %collective-permute-done.5 = f32[64,1024]{1,0:T(8,128)S(1)} collective-permute-done((f32[64,1024]{1,0:T(8,128)}, f32[64,1024]{1,0:T(8,128)S(1)}, u32[]{:S(2)}, u32[]{:S(2)}) %collective-permute-start.5) | collective-permute-done | bytes 262176 | tf_op jit(solution)/shard_map/ppermute | solution.py:56
  62.0 13.8 %collective-permute-done.3 = f32[64,1024]{1,0:T(8,128)S(1)} collective-permute-done((f32[64,1024]{1,0:T(8,128)}, f32[64,1024]{1,0:T(8,128)S(1)}, u32[]{:S(2)}, u32[]{:S(2)}) %collective-permute-start.3) | collective-permute-done | bytes 262176 | tf_op jit(solution)/shard_map/ppermute | solution.py:56
  75.8 3.7 %collective-permute-done.2 = f32[64,1024]{1,0:T(8,128)} collective-permute-done((f32[64,1024]{1,0:T(8,128)S(1)}, f32[64,1024]{1,0:T(8,128)}, u32[]{:S(2)}, u32[]{:S(2)}) %collective-permute-start.2) | collective-permute-done | bytes 262176 | tf_op jit(solution)/shard_map/ppermute | solution.py:56
  79.5 1.2 add_add_fusion
  80.7 1.9 collective-permute-start.8
  82.6 6.6 %collective-permute-start.10 = (f32[16,1024]{1,0:T(8,128)S(1)}, f32[16,1024]{1,0:T(8,128)S(1)}, u32[]{:S(2)}, u32[]{:S(2)}) collective-permute-start(f32[16,1024]{1,0:T(8,128)S(1)} %get-tuple-element.15), channel_id=1, source_target_pairs={{0,384},{8,392},{16,400},{24,408},{32,416},{40,424},{48,432},{56,4... | collective-permute-start | bytes 196616 | tf_op jit(solution)/shard_map/ppermute | solution.py:63
  89.2 5.5 %collective-permute-start.9 = (f32[16,1024]{1,0:T(8,128)S(1)}, f32[16,1024]{1,0:T(8,128)S(1)}, u32[]{:S(2)}, u32[]{:S(2)}) collective-permute-start(f32[16,1024]{1,0:T(8,128)S(1)} %get-tuple-element.16), channel_id=1, source_target_pairs={{0,256},{8,264},{16,272},{24,280},{32,288},{40,296},{48,304},{56,3... | collective-permute-start | bytes 196616 | tf_op jit(solution)/shard_map/ppermute | solution.py:63
  94.7 3.4 %collective-permute-done.9 = f32[16,1024]{1,0:T(8,128)S(1)} collective-permute-done((f32[16,1024]{1,0:T(8,128)S(1)}, f32[16,1024]{1,0:T(8,128)S(1)}, u32[]{:S(2)}, u32[]{:S(2)}) %collective-permute-start.9) | collective-permute-done | bytes 65568 | tf_op jit(solution)/shard_map/ppermute | solution.py:63
  98.1 4.3 %collective-permute-start.11 = (bf16[16,1024]{1,0:T(8,128)(2,1)S(1)}, bf16[16,1024]{1,0:T(8,128)(2,1)S(1)}, u32[]{:S(2)}, u32[]{:S(2)}) collective-permute-start(bf16[16,1024]{1,0:T(8,128)(2,1)S(1)} %get-tuple-element.6), channel_id=1, source_target_pairs={{0,384},{8,392},{16,400},{24,408},{32,416},{40,424},{48,432},{56,4... | collective-permute-start | bytes 98312 | tf_op jit(solution)/shard_map/ppermute | solution.py:70
  102.4 1.9 collective-permute-start.13
  104.4 6.1 %collective-permute-start.12 = (bf16[16,1024]{1,0:T(8,128)(2,1)S(1)}, bf16[16,1024]{1,0:T(8,128)(2,1)S(1)}, u32[]{:S(2)}, u32[]{:S(2)}) collective-permute-start(bf16[16,1024]{1,0:T(8,128)(2,1)S(1)} %get-tuple-element.6), channel_id=1, source_target_pairs={{0,256},{8,264},{16,272},{24,280},{32,288},{40,296},{48,304},{56,3... | collective-permute-start | bytes 98312 | tf_op jit(solution)/shard_map/ppermute | solution.py:70
  110.5 2.4 collective-permute-done.12
  113.0 11.7 %collective-permute-start.14 = (bf16[64,1024]{1,0:T(8,128)(2,1)S(1)}, bf16[64,1024]{1,0:T(8,128)(2,1)S(1)}, u32[]{:S(2)}, u32[]{:S(2)}) collective-permute-start(bf16[64,1024]{1,0:T(8,128)(2,1)S(1)} %bitcast.83), channel_id=1, source_target_pairs={{0,112},{8,120},{16,0},{24,8},{32,16},{40,24},{48,32},{56,40},{64,... | collective-permute-start | bytes 393224 | tf_op jit(solution)/shard_map/ppermute | solution.py:70
  124.8 1.9 collective-permute-start.20
  126.7 2.2 collective-permute-start.19
  129.0 4.2 %collective-permute-start.18 = (bf16[64,1024]{1,0:T(8,128)(2,1)S(1)}, bf16[64,1024]{1,0:T(8,128)(2,1)S(1)}, u32[]{:S(2)}, u32[]{:S(2)}) collective-permute-start(bf16[64,1024]{1,0:T(8,128)(2,1)S(1)} %bitcast.86), channel_id=1, source_target_pairs={{0,48},{8,56},{16,64},{24,72},{32,80},{40,88},{48,96},{56,104},{64... | collective-permute-start | bytes 393224 | tf_op jit(solution)/shard_map/ppermute | solution.py:70
  133.2 5.3 %collective-permute-start.17 = (bf16[64,1024]{1,0:T(8,128)(2,1)S(1)}, bf16[64,1024]{1,0:T(8,128)(2,1)S(1)}, u32[]{:S(2)}, u32[]{:S(2)}) collective-permute-start(bf16[64,1024]{1,0:T(8,128)(2,1)S(1)} %bitcast.87), channel_id=1, source_target_pairs={{0,64},{8,72},{16,80},{24,88},{32,96},{40,104},{48,112},{56,120},{... | collective-permute-start | bytes 393224 | tf_op jit(solution)/shard_map/ppermute | solution.py:70
  138.5 5.2 %collective-permute-start.15 = (bf16[64,1024]{1,0:T(8,128)(2,1)S(1)}, bf16[64,1024]{1,0:T(8,128)(2,1)S(1)}, u32[]{:S(2)}, u32[]{:S(2)}) collective-permute-start(bf16[64,1024]{1,0:T(8,128)(2,1)S(1)} %bitcast.89), channel_id=1, source_target_pairs={{0,96},{8,104},{16,112},{24,120},{32,0},{40,8},{48,16},{56,24},{64... | collective-permute-start | bytes 393224 | tf_op jit(solution)/shard_map/ppermute | solution.py:70
  143.7 5.1 %collective-permute-done.15 = bf16[64,1024]{1,0:T(8,128)(2,1)S(1)} collective-permute-done((bf16[64,1024]{1,0:T(8,128)(2,1)S(1)}, bf16[64,1024]{1,0:T(8,128)(2,1)S(1)}, u32[]{:S(2)}, u32[]{:S(2)}) %collective-permute-start.15) | collective-permute-done | bytes 131104 | tf_op jit(solution)/shard_map/ppermute | solution.py:70
  148.8 2.8 collective-permute-start.16
  151.6 5.2 %collective-permute-done.16 = bf16[64,1024]{1,0:T(8,128)(2,1)S(1)} collective-permute-done((bf16[64,1024]{1,0:T(8,128)(2,1)S(1)}, bf16[64,1024]{1,0:T(8,128)(2,1)S(1)}, u32[]{:S(2)}, u32[]{:S(2)}) %collective-permute-start.16) | collective-permute-done | bytes 131104 | tf_op jit(solution)/shard_map/ppermute | solution.py:70
  157.1 0.1 constant_dynamic-slice_fusion
  157.2 8.8 %collective-permute-start.21 = (bf16[512,1024]{1,0:T(8,128)(2,1)S(1)}, bf16[512,1024]{1,0:T(8,128)(2,1)}, u32[]{:S(2)}, u32[]{:S(2)}) collective-permute-start(bf16[512,1024]{1,0:T(8,128)(2,1)S(1)} %bitcast.79), channel_id=1, source_target_pairs={{0,8},{8,0},{16,24},{24,16},{32,40},{40,32},{48,56},{56,48},{64,72... | collective-permute-start | bytes 3145736 | tf_op jit(solution)/shard_map/ppermute | solution.py:70
  166.0 2.2 collective-permute-done.21
  168.2 3.0 %fusion.12 = bf16[2,512,1024]{2,1,0:T(8,128)(2,1)S(1)} fusion(s32[]{:T(128)S(6)} %select_n.157, bf16[1,512,1024]{2,1,0:T(8,128)(2,1)S(1)} %bitcast.80, bf16[1,512,1024]{2,1,0:T(8,128)(2,1)} %bitcast.15), kind=kLoop, calls=%fused_computation.32 | loop fusion | flops 3145728 | bytes 4194308 | tf_op jit(solution)/shard_map/concatenate | solution.py:72
  171.3 5.0 %fusion.8 = (f32[]{:T(128)}, f32[1024,1024,1]{1,0,2:T(8,128)}) fusion(bf16[2,512,1024]{2,1,0:T(8,128)(2,1)S(1)} %fusion.12), kind=kOutput, calls=%fused_computation.18 | convolution fusion | flops 2149580800 | bytes 6291460 | tf_op jit(solution)/shard_map/dot_general | solution.py:83
  176.2 5.0 %multiply_reduce_fusion.1 = (f32[]{:T(128)}, f32[1024,1024]{1,0:T(8,128)}) fusion(bf16[1024,1024]{1,0:T(8,128)(2,1)S(1)} %bitcast.81), kind=kOutput, calls=%fused_computation.28 | convolution fusion | flops 2149580800 | bytes 6291460 | tf_op jit(solution)/shard_map/dot_general | solution.py:80
  181.9 10.7 %reduce-precision_convert_fusion.4 = bf16[1024,1024]{1,0:T(8,128)(2,1)} fusion(f32[1024,1024]{1,0:T(8,128)} %get-tuple-element.18, f32[]{:T(128)S(6)} %sqrt.12), kind=kOutput, calls=%fused_computation.25 | convolution fusion | flops 4316987392 | bytes 6291460 | tf_op jit(solution)/shard_map/dot_general | solution.py:29
  192.6 6.5 %reduce-precision_convert_fusion.3 = bf16[1024,1024]{1,0:T(8,128)(2,1)} fusion(bf16[1024,1024]{1,0:T(8,128)(2,1)} %reduce-precision_convert_fusion.4, f32[1024,1024]{1,0:T(8,128)} %get-tuple-element.18, f32[]{:T(128)S(6)} %sqrt.12), kind=kOutput, calls=%fused_computation.24 | convolution fusion | flops 2156920832 | bytes 8388612 | tf_op jit(solution)/shard_map/dot_general | solution.py:29
  199.1 10.2 %fusion.30 = bf16[1024,1024]{1,0:T(8,128)(2,1)} fusion(bf16[1024,1024]{1,0:T(8,128)(2,1)} %reduce-precision_convert_fusion.3, f32[1024,1024]{1,0:T(8,128)} %get-tuple-element.18, f32[]{:T(128)S(6)} %sqrt.12), kind=kOutput, calls=%fused_computation.42 | convolution fusion | flops 4315938816 | bytes 8388612 | tf_op jit(solution)/shard_map/dot_general | solution.py:90
  209.9 10.7 %reduce-precision_convert_fusion.1 = bf16[1024,1024]{1,0:T(8,128)(2,1)} fusion(f32[1024,1024,1]{1,0,2:T(8,128)} %get-tuple-element.20, f32[]{:T(128)S(6)} %sqrt.13), kind=kOutput, calls=%fused_computation.22 | convolution fusion | flops 4316987392 | bytes 6291460 | tf_op jit(solution)/shard_map/dot_general | solution.py:29
  220.6 9.3 %fusion.16 = bf16[1024,1024]{1,0:T(8,128)(2,1)} fusion(bf16[1024,1024]{1,0:T(8,128)(2,1)} %bitcast.82, bf16[1024,1024]{1,0:T(8,128)(2,1)} %fusion.30, f32[]{:T(128)S(6)} %sqrt.13, f32[1024,1024,1]{1,0,2:T(8,128)} %get-tuple-element.20), kind=kOutput, calls=%fused_computation.36 | convolution fusion | flops 4303355904 | bytes 10485764 | tf_op jit(solution)/shard_map/dot_general | solution.py:93
  229.9 6.9 %reduce-precision_convert_fusion = bf16[1024,1024]{1,0:T(8,128)(2,1)} fusion(bf16[1024,1024]{1,0:T(8,128)(2,1)} %reduce-precision_convert_fusion.1, f32[]{:T(128)S(6)} %sqrt.13, f32[1024,1024,1]{1,0,2:T(8,128)} %get-tuple-element.20), kind=kOutput, calls=%fused_computation.21 | convolution fusion | flops 2156920832 | bytes 8388612 | tf_op jit(solution)/shard_map/dot_general | solution.py:29
  236.8 10.7 %multiply_reduce_fusion = (f32[]{:T(128)}, f32[1024,1024]{1,0:T(8,128)}) fusion(bf16[1024,1024]{1,0:T(8,128)(2,1)} %fusion.16, bf16[1024,1024]{1,0:T(8,128)(2,1)} %reduce-precision_convert_fusion, f32[]{:T(128)S(6)} %sqrt.13, f32[1024,1024,1]{1,0,2:T(8,128)} %get-tuple-element.20), kind=kOutput, calls=%fused_computation.20 | convolution fusion | flops 4310695936 | bytes 12582920 | tf_op jit(solution)/shard_map/dot_general | solution.py:94
  247.4 0.6 broadcast_in_dim.3
  248.1 4.1 %collective-permute-start.27 = (f32[8,128]{1,0:T(8,128)S(1)}, f32[8,128]{1,0:T(8,128)S(1)}, u32[]{:S(2)}, u32[]{:S(2)}) collective-permute-start(f32[8,128]{1,0:T(8,128)S(1)} %broadcast_in_dim.3), channel_id=1, source_target_pairs={{0,6},{1,7},{2,0},{3,1},{4,2},{5,3},{6,4},{7,5},{8,14},{9,15},{10,... | collective-permute-start | bytes 12296 | tf_op jit(solution)/shard_map/ppermute | solution.py:99
  252.2 6.8 %collective-permute-start.26 = (f32[8,128]{1,0:T(8,128)S(1)}, f32[8,128]{1,0:T(8,128)S(1)}, u32[]{:S(2)}, u32[]{:S(2)}) collective-permute-start(f32[8,128]{1,0:T(8,128)S(1)} %broadcast_in_dim.3), channel_id=1, source_target_pairs={{0,5},{1,6},{2,7},{3,0},{4,1},{5,2},{6,3},{7,4},{8,13},{9,14},{10,... | collective-permute-start | bytes 12296 | tf_op jit(solution)/shard_map/ppermute | solution.py:99
  259.0 4.6 %collective-permute-start.25 = (f32[8,128]{1,0:T(8,128)S(1)}, f32[8,128]{1,0:T(8,128)S(1)}, u32[]{:S(2)}, u32[]{:S(2)}) collective-permute-start(f32[8,128]{1,0:T(8,128)S(1)} %broadcast_in_dim.3), channel_id=1, source_target_pairs={{0,4},{1,5},{2,6},{3,7},{4,0},{5,1},{6,2},{7,3},{8,12},{9,13},{10,... | collective-permute-start | bytes 12296 | tf_op jit(solution)/shard_map/ppermute | solution.py:99
  263.6 1.9 collective-permute-start.24
  265.6 1.9 collective-permute-start.23
  267.5 5.7 %collective-permute-start.28 = (f32[8,128]{1,0:T(8,128)S(1)}, f32[8,128]{1,0:T(8,128)S(1)}, u32[]{:S(2)}, u32[]{:S(2)}) collective-permute-start(f32[8,128]{1,0:T(8,128)S(1)} %broadcast_in_dim.3), channel_id=1, source_target_pairs={{0,7},{1,0},{2,1},{3,2},{4,3},{5,4},{6,5},{7,6},{8,15},{9,8},{10,9... | collective-permute-start | bytes 12296 | tf_op jit(solution)/shard_map/ppermute | solution.py:99
  273.3 1.9 collective-permute-start.22
  275.2 4.5 %collective-permute-done.22 = f32[8,128]{1,0:T(8,128)S(1)} collective-permute-done((f32[8,128]{1,0:T(8,128)S(1)}, f32[8,128]{1,0:T(8,128)S(1)}, u32[]{:S(2)}, u32[]{:S(2)}) %collective-permute-start.22) | collective-permute-done | bytes 4128 | tf_op jit(solution)/shard_map/ppermute | solution.py:99
  279.7 0.7 add_add_fusion.1
  280.4 0.5 slice.3
  281.6 1.5 divide_convert_fusion
  (48 shorter events, 0.3 us)
Async XLA Ops:
  0.0 1.4 copy-start
  4.7 2.0 copy-start.2
  8.2 12.9 %collective-permute-start = (f32[512,1024]{1,0:T(8,128)}, f32[512,1024]{1,0:T(8,128)}, u32[]{:S(2)}, u32[]{:S(2)}) collective-permute-start(f32[512,1024]{1,0:T(8,128)} %constant_dynamic-slice_fusion.12), channel_id=1, source_target_pairs={{0,8},{8,0},{16,24},{24,16},{32,40},{40,32},{48,56},{56,48},{64,72... | collective-permute-start | bytes 6291464 | tf_op jit(solution)/shard_map/ppermute | solution.py:52
  23.7 1.4 copy-start.1
  26.1 17.6 %collective-permute-start.1 = (f32[64,1024]{1,0:T(8,128)S(1)}, f32[64,1024]{1,0:T(8,128)S(1)}, u32[]{:S(2)}, u32[]{:S(2)}) collective-permute-start(f32[64,1024]{1,0:T(8,128)S(1)} %get-tuple-element.7), channel_id=1, source_target_pairs={{0,16},{8,24},{16,32},{24,40},{32,48},{40,56},{48,64},{56,72},{64,... | collective-permute-start | bytes 786440 | tf_op jit(solution)/shard_map/ppermute | solution.py:56
  28.0 17.7 %collective-permute-start.7 = (f32[64,1024]{1,0:T(8,128)S(1)}, f32[64,1024]{1,0:T(8,128)S(1)}, u32[]{:S(2)}, u32[]{:S(2)}) collective-permute-start(f32[64,1024]{1,0:T(8,128)S(1)} %get-tuple-element.8), channel_id=1, source_target_pairs={{0,112},{8,120},{16,0},{24,8},{32,16},{40,24},{48,32},{56,40},{64,... | collective-permute-start | bytes 786440 | tf_op jit(solution)/shard_map/ppermute | solution.py:56
  32.6 18.0 %collective-permute-start.6 = (f32[64,1024]{1,0:T(8,128)}, f32[64,1024]{1,0:T(8,128)S(1)}, u32[]{:S(2)}, u32[]{:S(2)}) collective-permute-start(f32[64,1024]{1,0:T(8,128)} %get-tuple-element.9), channel_id=1, source_target_pairs={{0,96},{8,104},{16,112},{24,120},{32,0},{40,8},{48,16},{56,24},{64... | collective-permute-start | bytes 786440 | tf_op jit(solution)/shard_map/ppermute | solution.py:56
  34.5 27.5 %collective-permute-start.5 = (f32[64,1024]{1,0:T(8,128)}, f32[64,1024]{1,0:T(8,128)S(1)}, u32[]{:S(2)}, u32[]{:S(2)}) collective-permute-start(f32[64,1024]{1,0:T(8,128)} %get-tuple-element.10), channel_id=1, source_target_pairs={{0,80},{8,88},{16,96},{24,104},{32,112},{40,120},{48,0},{56,8},{64... | collective-permute-start | bytes 786440 | tf_op jit(solution)/shard_map/ppermute | solution.py:56
  36.6 25.4 %collective-permute-start.4 = (f32[64,1024]{1,0:T(8,128)}, f32[64,1024]{1,0:T(8,128)S(1)}, u32[]{:S(2)}, u32[]{:S(2)}) collective-permute-start(f32[64,1024]{1,0:T(8,128)} %get-tuple-element.11), channel_id=1, source_target_pairs={{0,64},{8,72},{16,80},{24,88},{32,96},{40,104},{48,112},{56,120},{... | collective-permute-start | bytes 786440 | tf_op jit(solution)/shard_map/ppermute | solution.py:56
  43.7 32.1 %collective-permute-start.3 = (f32[64,1024]{1,0:T(8,128)}, f32[64,1024]{1,0:T(8,128)S(1)}, u32[]{:S(2)}, u32[]{:S(2)}) collective-permute-start(f32[64,1024]{1,0:T(8,128)} %get-tuple-element.12), channel_id=1, source_target_pairs={{0,48},{8,56},{16,64},{24,72},{32,80},{40,88},{48,96},{56,104},{64... | collective-permute-start | bytes 786440 | tf_op jit(solution)/shard_map/ppermute | solution.py:56
  45.6 33.8 %collective-permute-start.2 = (f32[64,1024]{1,0:T(8,128)S(1)}, f32[64,1024]{1,0:T(8,128)}, u32[]{:S(2)}, u32[]{:S(2)}) collective-permute-start(f32[64,1024]{1,0:T(8,128)S(1)} %get-tuple-element.13), channel_id=1, source_target_pairs={{0,32},{8,40},{16,48},{24,56},{32,64},{40,72},{48,80},{56,88},{64,... | collective-permute-start | bytes 786440 | tf_op jit(solution)/shard_map/ppermute | solution.py:56
  80.7 14.0 %collective-permute-start.8 = (f32[16,1024]{1,0:T(8,128)S(1)}, f32[16,1024]{1,0:T(8,128)S(1)}, u32[]{:S(2)}, u32[]{:S(2)}) collective-permute-start(f32[16,1024]{1,0:T(8,128)S(1)} %get-tuple-element.14), channel_id=1, source_target_pairs={{0,128},{8,136},{16,144},{24,152},{32,160},{40,168},{48,176},{56,1... | collective-permute-start | bytes 196616 | tf_op jit(solution)/shard_map/ppermute | solution.py:63
  82.6 12.1 %collective-permute-start.10 = (f32[16,1024]{1,0:T(8,128)S(1)}, f32[16,1024]{1,0:T(8,128)S(1)}, u32[]{:S(2)}, u32[]{:S(2)}) collective-permute-start(f32[16,1024]{1,0:T(8,128)S(1)} %get-tuple-element.15), channel_id=1, source_target_pairs={{0,384},{8,392},{16,400},{24,408},{32,416},{40,424},{48,432},{56,4... | collective-permute-start | bytes 196616 | tf_op jit(solution)/shard_map/ppermute | solution.py:63
  89.2 8.9 %collective-permute-start.9 = (f32[16,1024]{1,0:T(8,128)S(1)}, f32[16,1024]{1,0:T(8,128)S(1)}, u32[]{:S(2)}, u32[]{:S(2)}) collective-permute-start(f32[16,1024]{1,0:T(8,128)S(1)} %get-tuple-element.16), channel_id=1, source_target_pairs={{0,256},{8,264},{16,272},{24,280},{32,288},{40,296},{48,304},{56,3... | collective-permute-start | bytes 196616 | tf_op jit(solution)/shard_map/ppermute | solution.py:63
  98.1 12.4 %collective-permute-start.11 = (bf16[16,1024]{1,0:T(8,128)(2,1)S(1)}, bf16[16,1024]{1,0:T(8,128)(2,1)S(1)}, u32[]{:S(2)}, u32[]{:S(2)}) collective-permute-start(bf16[16,1024]{1,0:T(8,128)(2,1)S(1)} %get-tuple-element.6), channel_id=1, source_target_pairs={{0,384},{8,392},{16,400},{24,408},{32,416},{40,424},{48,432},{56,4... | collective-permute-start | bytes 98312 | tf_op jit(solution)/shard_map/ppermute | solution.py:70
  102.4 10.5 %collective-permute-start.13 = (bf16[16,1024]{1,0:T(8,128)(2,1)S(1)}, bf16[16,1024]{1,0:T(8,128)(2,1)S(1)}, u32[]{:S(2)}, u32[]{:S(2)}) collective-permute-start(bf16[16,1024]{1,0:T(8,128)(2,1)S(1)} %get-tuple-element.6), channel_id=1, source_target_pairs={{0,128},{8,136},{16,144},{24,152},{32,160},{40,168},{48,176},{56,1... | collective-permute-start | bytes 98312 | tf_op jit(solution)/shard_map/ppermute | solution.py:70
  104.4 8.6 %collective-permute-start.12 = (bf16[16,1024]{1,0:T(8,128)(2,1)S(1)}, bf16[16,1024]{1,0:T(8,128)(2,1)S(1)}, u32[]{:S(2)}, u32[]{:S(2)}) collective-permute-start(bf16[16,1024]{1,0:T(8,128)(2,1)S(1)} %get-tuple-element.6), channel_id=1, source_target_pairs={{0,256},{8,264},{16,272},{24,280},{32,288},{40,296},{48,304},{56,3... | collective-permute-start | bytes 98312 | tf_op jit(solution)/shard_map/ppermute | solution.py:70
  113.0 25.4 %collective-permute-start.14 = (bf16[64,1024]{1,0:T(8,128)(2,1)S(1)}, bf16[64,1024]{1,0:T(8,128)(2,1)S(1)}, u32[]{:S(2)}, u32[]{:S(2)}) collective-permute-start(bf16[64,1024]{1,0:T(8,128)(2,1)S(1)} %bitcast.83), channel_id=1, source_target_pairs={{0,112},{8,120},{16,0},{24,8},{32,16},{40,24},{48,32},{56,40},{64,... | collective-permute-start | bytes 393224 | tf_op jit(solution)/shard_map/ppermute | solution.py:70
  124.8 32.1 %collective-permute-start.20 = (bf16[64,1024]{1,0:T(8,128)(2,1)S(1)}, bf16[64,1024]{1,0:T(8,128)(2,1)S(1)}, u32[]{:S(2)}, u32[]{:S(2)}) collective-permute-start(bf16[64,1024]{1,0:T(8,128)(2,1)S(1)} %bitcast.84), channel_id=1, source_target_pairs={{0,16},{8,24},{16,32},{24,40},{32,48},{40,56},{48,64},{56,72},{64,... | collective-permute-start | bytes 393224 | tf_op jit(solution)/shard_map/ppermute | solution.py:70
  126.7 30.2 %collective-permute-start.19 = (bf16[64,1024]{1,0:T(8,128)(2,1)S(1)}, bf16[64,1024]{1,0:T(8,128)(2,1)S(1)}, u32[]{:S(2)}, u32[]{:S(2)}) collective-permute-start(bf16[64,1024]{1,0:T(8,128)(2,1)S(1)} %bitcast.85), channel_id=1, source_target_pairs={{0,32},{8,40},{16,48},{24,56},{32,64},{40,72},{48,80},{56,88},{64,... | collective-permute-start | bytes 393224 | tf_op jit(solution)/shard_map/ppermute | solution.py:70
  129.0 27.9 %collective-permute-start.18 = (bf16[64,1024]{1,0:T(8,128)(2,1)S(1)}, bf16[64,1024]{1,0:T(8,128)(2,1)S(1)}, u32[]{:S(2)}, u32[]{:S(2)}) collective-permute-start(bf16[64,1024]{1,0:T(8,128)(2,1)S(1)} %bitcast.86), channel_id=1, source_target_pairs={{0,48},{8,56},{16,64},{24,72},{32,80},{40,88},{48,96},{56,104},{64... | collective-permute-start | bytes 393224 | tf_op jit(solution)/shard_map/ppermute | solution.py:70
  133.2 23.7 %collective-permute-start.17 = (bf16[64,1024]{1,0:T(8,128)(2,1)S(1)}, bf16[64,1024]{1,0:T(8,128)(2,1)S(1)}, u32[]{:S(2)}, u32[]{:S(2)}) collective-permute-start(bf16[64,1024]{1,0:T(8,128)(2,1)S(1)} %bitcast.87), channel_id=1, source_target_pairs={{0,64},{8,72},{16,80},{24,88},{32,96},{40,104},{48,112},{56,120},{... | collective-permute-start | bytes 393224 | tf_op jit(solution)/shard_map/ppermute | solution.py:70
  138.5 10.3 %collective-permute-start.15 = (bf16[64,1024]{1,0:T(8,128)(2,1)S(1)}, bf16[64,1024]{1,0:T(8,128)(2,1)S(1)}, u32[]{:S(2)}, u32[]{:S(2)}) collective-permute-start(bf16[64,1024]{1,0:T(8,128)(2,1)S(1)} %bitcast.89), channel_id=1, source_target_pairs={{0,96},{8,104},{16,112},{24,120},{32,0},{40,8},{48,16},{56,24},{64... | collective-permute-start | bytes 393224 | tf_op jit(solution)/shard_map/ppermute | solution.py:70
  148.8 8.1 %collective-permute-start.16 = (bf16[64,1024]{1,0:T(8,128)(2,1)S(1)}, bf16[64,1024]{1,0:T(8,128)(2,1)S(1)}, u32[]{:S(2)}, u32[]{:S(2)}) collective-permute-start(bf16[64,1024]{1,0:T(8,128)(2,1)S(1)} %bitcast.90), channel_id=1, source_target_pairs={{0,80},{8,88},{16,96},{24,104},{32,112},{40,120},{48,0},{56,8},{64... | collective-permute-start | bytes 393224 | tf_op jit(solution)/shard_map/ppermute | solution.py:70
  157.2 11.0 %collective-permute-start.21 = (bf16[512,1024]{1,0:T(8,128)(2,1)S(1)}, bf16[512,1024]{1,0:T(8,128)(2,1)}, u32[]{:S(2)}, u32[]{:S(2)}) collective-permute-start(bf16[512,1024]{1,0:T(8,128)(2,1)S(1)} %bitcast.79), channel_id=1, source_target_pairs={{0,8},{8,0},{16,24},{24,16},{32,40},{40,32},{48,56},{56,48},{64,72... | collective-permute-start | bytes 3145736 | tf_op jit(solution)/shard_map/ppermute | solution.py:70
  171.3 5.0 %copy-start.3 = (bf16[2,512,1024]{2,1,0:T(8,128)(2,1)}, bf16[2,512,1024]{2,1,0:T(8,128)(2,1)S(1)}, u32[]{:S(2)}) copy-start(bf16[2,512,1024]{2,1,0:T(8,128)(2,1)S(1)} %fusion.12) | copy-start | bytes 6291460
  248.1 19.4 %collective-permute-start.27 = (f32[8,128]{1,0:T(8,128)S(1)}, f32[8,128]{1,0:T(8,128)S(1)}, u32[]{:S(2)}, u32[]{:S(2)}) collective-permute-start(f32[8,128]{1,0:T(8,128)S(1)} %broadcast_in_dim.3), channel_id=1, source_target_pairs={{0,6},{1,7},{2,0},{3,1},{4,2},{5,3},{6,4},{7,5},{8,14},{9,15},{10,... | collective-permute-start | bytes 12296 | tf_op jit(solution)/shard_map/ppermute | solution.py:99
  252.2 21.0 %collective-permute-start.26 = (f32[8,128]{1,0:T(8,128)S(1)}, f32[8,128]{1,0:T(8,128)S(1)}, u32[]{:S(2)}, u32[]{:S(2)}) collective-permute-start(f32[8,128]{1,0:T(8,128)S(1)} %broadcast_in_dim.3), channel_id=1, source_target_pairs={{0,5},{1,6},{2,7},{3,0},{4,1},{5,2},{6,3},{7,4},{8,13},{9,14},{10,... | collective-permute-start | bytes 12296 | tf_op jit(solution)/shard_map/ppermute | solution.py:99
  259.0 16.2 %collective-permute-start.25 = (f32[8,128]{1,0:T(8,128)S(1)}, f32[8,128]{1,0:T(8,128)S(1)}, u32[]{:S(2)}, u32[]{:S(2)}) collective-permute-start(f32[8,128]{1,0:T(8,128)S(1)} %broadcast_in_dim.3), channel_id=1, source_target_pairs={{0,4},{1,5},{2,6},{3,7},{4,0},{5,1},{6,2},{7,3},{8,12},{9,13},{10,... | collective-permute-start | bytes 12296 | tf_op jit(solution)/shard_map/ppermute | solution.py:99
  263.6 11.6 %collective-permute-start.24 = (f32[8,128]{1,0:T(8,128)S(1)}, f32[8,128]{1,0:T(8,128)S(1)}, u32[]{:S(2)}, u32[]{:S(2)}) collective-permute-start(f32[8,128]{1,0:T(8,128)S(1)} %broadcast_in_dim.3), channel_id=1, source_target_pairs={{0,3},{1,4},{2,5},{3,6},{4,7},{5,0},{6,1},{7,2},{8,11},{9,12},{10,... | collective-permute-start | bytes 12296 | tf_op jit(solution)/shard_map/ppermute | solution.py:99
  265.6 9.6 %collective-permute-start.23 = (f32[8,128]{1,0:T(8,128)S(1)}, f32[8,128]{1,0:T(8,128)S(1)}, u32[]{:S(2)}, u32[]{:S(2)}) collective-permute-start(f32[8,128]{1,0:T(8,128)S(1)} %broadcast_in_dim.3), channel_id=1, source_target_pairs={{0,2},{1,3},{2,4},{3,5},{4,6},{5,7},{6,0},{7,1},{8,10},{9,11},{10,... | collective-permute-start | bytes 12296 | tf_op jit(solution)/shard_map/ppermute | solution.py:99
  267.5 7.7 %collective-permute-start.28 = (f32[8,128]{1,0:T(8,128)S(1)}, f32[8,128]{1,0:T(8,128)S(1)}, u32[]{:S(2)}, u32[]{:S(2)}) collective-permute-start(f32[8,128]{1,0:T(8,128)S(1)} %broadcast_in_dim.3), channel_id=1, source_target_pairs={{0,7},{1,0},{2,1},{3,2},{4,3},{5,4},{6,5},{7,6},{8,15},{9,8},{10,9... | collective-permute-start | bytes 12296 | tf_op jit(solution)/shard_map/ppermute | solution.py:99
  273.3 6.5 %collective-permute-start.22 = (f32[8,128]{1,0:T(8,128)S(1)}, f32[8,128]{1,0:T(8,128)S(1)}, u32[]{:S(2)}, u32[]{:S(2)}) collective-permute-start(f32[8,128]{1,0:T(8,128)S(1)} %broadcast_in_dim.3), channel_id=1, source_target_pairs={{0,1},{1,2},{2,3},{3,4},{4,5},{5,6},{6,7},{7,0},{8,9},{9,10},{10,1... | collective-permute-start | bytes 12296 | tf_op jit(solution)/shard_map/ppermute | solution.py:99

commit v2 on v0

v2 whole, which is shorter than its diff:
```python
import jax
import jax.numpy as jnp
import numpy as np
from jax import lax
from jax.experimental import pallas as pl
from jax.experimental.pallas import tpu as pltpu
from jax.sharding import Mesh, PartitionSpec as P

Z, Y, C = 4, 8, 2
DP = ("z", "y", "c")
TILE = 256
VMEM = pl.BlockSpec(memory_space=pltpu.VMEM)
SMEM = pl.BlockSpec(memory_space=pltpu.SMEM)
f32, bf16 = jnp.float32, jnp.bfloat16


def device(z, y, c):
    return z * Y * C + y * C + c


FIRST = [[device(z, y, 0) for y in range(Y)] for z in range(Z)] + [
    [device(z, 2 * p + q, 1) for z in range(Z) for q in range(2)] for p in range(Y // 2)
]
SECOND = [[device(z, y, 0) for z in range(Z)] for y in range(Y)] + [
    [device(z, 2 * p + q, 1) for p in range(Y // 2)] for z in range(Z) for q in range(2)
]


def half_product(half, tokens, cotangent):
    depth, width = tokens.shape
    rows = width // C

    def body(half_ref, tokens_ref, cotangent_ref, out_ref, turned):
        turned[...] = tokens_ref[...].T

        @pl.loop(0, width // TILE)
        def _(n):
            columns = pl.ds(pl.multiple_of(n * TILE, TILE), TILE)
            out_ref[:, columns] = jnp.dot(
                turned[...], cotangent_ref[:, columns], preferred_element_type=f32
            )

    return pl.pallas_call(
        body,
        grid_spec=pltpu.PrefetchScalarGridSpec(
            num_scalar_prefetch=1,
            grid=(1,),
            in_specs=[
                pl.BlockSpec((depth, rows), lambda i, half: (0, half[0])),
                pl.BlockSpec((depth, width), lambda i, half: (0, 0)),
            ],
            out_specs=pl.BlockSpec((rows, width), lambda i, half: (0, 0)),
            scratch_shapes=[pltpu.VMEM((rows, depth), bf16)],
        ),
        out_shape=jax.ShapeDtypeStruct((rows, width), f32),
        compiler_params=pltpu.CompilerParams(vmem_limit_bytes=40 * 2**20),
        cost_estimate=pl.CostEstimate(
            flops=2 * depth * rows * width, bytes_accessed=6 * 2**20, transcendentals=0
        ),
        name="half_product",
    )(half, tokens, cotangent)


def precondition(place, mine, theirs):
    half, width = mine.shape
    block = 16
    tiles = width // TILE

    def body(place_ref, mine_ref, theirs_ref, rows_ref, square_ref, g, gt, sl, sr, xl, yl, xr, yr, f0l, f1l, f0r, f1r, h, k):
        core, own = place_ref[0], place_ref[1]
        g[pl.ds(pl.multiple_of(core * half, half), half), :] = mine_ref[...]
        g[pl.ds(pl.multiple_of((1 - core) * half, half), half), :] = theirs_ref[...]

        def at(n):
            return pl.ds(pl.multiple_of(n * TILE, TILE), TILE)

        def fold(square):
            return jnp.sum(square.reshape(-1, 8, square.shape[1]), axis=0)

        def identity(n):
            row = lax.broadcasted_iota(jnp.int32, (width, TILE), 0)
            column = lax.broadcasted_iota(jnp.int32, (width, TILE), 1)
            return row == column + n * TILE

        def factor(iterate, eye):
            return (jnp.where(eye, 5.0 - iterate, -iterate) * 0.25).astype(bf16)

        def stat(a, b, out, n, acc):
            s = jnp.dot(a[...], b[:, at(n)], preferred_element_type=f32)
            out[:, at(n)] = s
            return acc + fold(s * s)

        def first(s, inverse, x, f, n):
            it = (s[:, at(n)] * inverse).astype(bf16)
            x[:, at(n)] = it
            f[:, at(n)] = factor(it.astype(f32), identity(n))

        def power(x, f, out, n):
            out[:, at(n)] = jnp.dot(x[...], f[:, at(n)], preferred_element_type=f32).astype(bf16)

        def last(x, f, out, n):
            it = jnp.dot(x[...], f[:, at(n)], preferred_element_type=f32).astype(bf16)
            out[:, at(n)] = factor(it.astype(f32), identity(n))

        def inverse_norm(acc):
            total = jnp.sum(jnp.sum(acc, axis=0, keepdims=True), axis=1, keepdims=True)
            return 1.0 / jnp.sqrt(total)

        zero = jnp.zeros((8, TILE), f32)

        @pl.loop(0, tiles)
        def _(n):
            gt[:, at(n)] = g[at(n), :].T

        acc = lax.fori_loop(0, tiles, lambda n, a: stat(g, gt, sl, n, a), zero)
        inverse_l = inverse_norm(acc)

        def both(n, a):
            first(sl, inverse_l, xl, f0l, n)
            return stat(gt, g, sr, n, a)

        inverse_r = inverse_norm(lax.fori_loop(0, tiles, both, zero))

        @pl.loop(0, tiles)
        def _(n):
            first(sr, inverse_r, xr, f0r, n)
            power(xl, f0l, yl, n)

        @pl.loop(0, tiles)
        def _(n):
            power(yl, f0l, xl, n)
            power(xr, f0r, yr, n)

        @pl.loop(0, tiles)
        def _(n):
            power(xl, f0l, yl, n)
            power(yr, f0r, xr, n)

        @pl.loop(0, tiles)
        def _(n):
            last(yl, f0l, f1l, n)
            power(xr, f0r, yr, n)

        @pl.loop(0, half // block)
        def _(i):
            source = pl.ds(pl.multiple_of((2 * i + core) * block, block), block)
            h[pl.ds(pl.multiple_of(i * block, block), block), :] = f0l[source, :]

        @pl.loop(0, tiles)
        def _(n):
            last(yr, f0r, f1r, n)
            power(h, f1l, k, n)

        @pl.loop(0, tiles)
        def _(n):
            power(k, g, h, n)

        @pl.loop(0, tiles)
        def _(n):
            power(h, f0r, k, n)

        precond = sl

        def final(n, a):
            p = jnp.dot(k[...], f1r[:, at(n)], preferred_element_type=f32)
            precond[pl.ds(0, half), at(n)] = p
            return a + fold(p * p)

        acc = lax.fori_loop(0, tiles, final, zero)
        square_ref[...] = acc[:, :128] + acc[:, 128:]
        rows_ref[...] = precond[pl.ds(pl.multiple_of(own * block, block), block), :]

    wide, stat_t = pltpu.VMEM((width, width), bf16), pltpu.VMEM((width, width), f32)
    narrow = pltpu.VMEM((half, width), bf16)
    return pl.pallas_call(
        body,
        in_specs=[SMEM, VMEM, VMEM],
        out_specs=[VMEM, VMEM],
        out_shape=[
            jax.ShapeDtypeStruct((block, width), f32),
            jax.ShapeDtypeStruct((8, 128), f32),
        ],
        scratch_shapes=[wide, wide, stat_t, stat_t] + [wide] * 8 + [narrow] * 2,
        compiler_params=pltpu.CompilerParams(vmem_limit_bytes=48 * 2**20),
        cost_estimate=pl.CostEstimate(
            flops=24 * width**3, bytes_accessed=3 * 2**20, transcendentals=0
        ),
        name="precondition",
    )(place, mine, theirs)


def on_device(tokens, cotangent):
    width = tokens.shape[1]
    z, y, c = lax.axis_index("z"), lax.axis_index("y"), lax.axis_index("c")
    half = width // C
    core_swap = [(0, 1), (1, 0)]

    near_half = jnp.full((1,), c, jnp.int32)
    away = half_product(1 - near_half, tokens, cotangent)
    received = lax.ppermute(away, "c", core_swap)
    near = half_product(near_half, tokens, cotangent)
    rows = near + received
    for groups in (FIRST, SECOND):
        count = len(groups[0])
        parts = rows.reshape(count, rows.shape[0] // count, width)
        rows = jnp.sum(lax.all_to_all(parts, DP, 0, 0, axis_index_groups=groups), axis=0)
    rows = rows.astype(bf16)
    for groups in (SECOND, FIRST):
        count = len(groups[0])
        copies = jnp.broadcast_to(rows, (count,) + rows.shape)
        rows = lax.all_to_all(copies, DP, 0, 0, axis_index_groups=groups)
        rows = rows.reshape(count * rows.shape[1], width)
    theirs = lax.ppermute(rows, "c", core_swap)

    place = jnp.stack([c, z * Y + y]).astype(jnp.int32)
    precond, square = precondition(place, rows, theirs)
    square = jnp.broadcast_to(jnp.sum(square), (C * lax.axis_size("group"), 1, 128))
    total = jnp.sum(lax.all_to_all(square, ("c", "group"), 0, 0)[:, 0, 0])
    mean_square = total / (lax.axis_size("group") * width * width)
    return (precond / jnp.sqrt(mean_square + 1e-06)).astype(bf16)


def solution(mesh):
    groups = mesh.shape["group"]
    split = Mesh(np.asarray(mesh.devices).reshape(Z, Y, C, groups), DP + ("group",))
    return jax.shard_map(
        on_device,
        mesh=split,
        in_specs=(P(DP, None), P(DP, "group")),
        out_specs=P(DP, "group"),
        check_vma=False,
    )
```

time: 854 us -> 173 us (0.20)
  waiting for transfers between devices: 561 us -> 4.13 us
  blocking collectives: 235 us -> 103 us
  Pallas kernels: 0 us -> 45 us
  matrix products: 33.9 us -> 0 us
  between operations: 15.6 us -> 0.8 us
  starting transfers between devices: 0.21 us -> 13.2 us
    all_gather x5 -> x0, waiting for transfers between devices: 403 us -> none  [the longest x2 158 us: on_device(): lax.all_gather(right_slab, 'dp', axis=0, tiled=True)]
    psum x2 -> x0, blocking collectives: 235 us -> none  [the longest x1 139 us: on_device(): lax.psum((jnp.sum(left_rows * left_rows), jnp.sum(right_rows * right_rows...]
    reduce_scatter x1 -> x0, waiting for transfers between devices: 158 us -> none  [on_device(): lax.psum_scatter(lax.dot_general(tokens, cotangent, (((0,), (0,)), ((), (...]
    all_to_all x0 -> x5, blocking collectives: none -> 103 us  [the longest x2 58.5 us: on_device(): lax.all_to_all(parts, DP, 0, 0, axis_index_groups=groups)]
    pallas_call x0 -> x3, Pallas kernels: none -> 45 us  [the longest x1 41.4 us: precondition(): pl.pallas_call(body, in_specs=[SMEM, VMEM, VMEM], out_specs=[VMEM, VMEM],...]
    dot_general x10 -> x0, matrix products: 33.9 us -> none  [the longest x2 7.34 us: on_device(): jnp.dot(left_slab, left_factor, preferred_element_type=jnp.float32)]
    ppermute x0 -> x2, starting transfers between devices: none -> 13.2 us  [the longest x1 8.79 us: on_device(): received = lax.ppermute(away, 'c', core_swap)]
  transfers between devices with their start and end apart: 6 -> 2, of which waited for: 6 -> 2; matrix products, arithmetic and copies ran while one was open for 3% -> 0% of each run, Pallas kernels for 0% -> 1%
where the time goes in v2:
time: 173 us; the launch traced here: 172 us
  blocking collectives  103 us (60%)
  Pallas kernels  45 us (26%)
  starting transfers between devices  13.2 us (8%)
  waiting for transfers between devices  4.13 us (2%)
  local copies, waits for them, and re-layouts  3.59 us (2%)
  other arithmetic  2.53 us (1%)
    all_to_all x2, blocking collectives, on_device(): lax.all_to_all(parts, DP, 0, 0, axis_index_groups=groups)  58.5 us
    pallas_call x1, Pallas kernels, precondition(): pl.pallas_call(body, in_specs=[SMEM, VMEM, VMEM], out_specs=[VMEM, VMEM],...  41.4 us
    all_to_all x2, blocking collectives, on_device(): rows = lax.all_to_all(copies, DP, 0, 0, axis_index_groups=groups)  34.4 us
    all_to_all x1, blocking collectives, on_device(): total = jnp.sum(lax.all_to_all(square, ('c', 'group'), 0, 0)[:, 0, 0])  9.98 us
    ppermute x1, starting transfers between devices, on_device(): received = lax.ppermute(away, 'c', core_swap)  8.79 us
    ppermute x1, starting transfers between devices, on_device(): theirs = lax.ppermute(rows, 'c', core_swap)  4.43 us
    pallas_call x2, Pallas kernels, half_product(): pl.pallas_call(body, grid_spec=pltpu.PrefetchScalarGridSpec(num_scalar_pr...  3.6 us
  transfers between devices with their start and end apart: 2, of which 2 were waited for; matrix products, arithmetic and copies ran while one was open for 0% of the time, Pallas kernels for 1%

profile of v2, /device:TPU:1, one launch (start us, length us, event | category | flops | bytes accessed | tf_op | source)
XLA Modules:
  0.0 172.2 jit_solution(15642302831915644000)
XLA Ops:
  0.0 0.0 copy-start
  0.0 1.4 copy-done
  1.4 0.0 copy-start.2
  1.4 1.4 copy-done.2
  2.8 0.0 copy-start.1
  2.8 1.8 %half_product.3 = f32[512,1024]{1,0:T(8,128)S(1)} custom-call(s32[1]{0:T(128)S(6)} %sub.3.half_ref, bf16[768,1024]{1,0:T(8,128)(2,1)S(1)} %copy-done, bf16[768,1024]{1,0:T(8,128)(2,1)S(1)} %copy-done.2), custom_call_target="tpu_custom_call" | custom-call | flops 805306368 | bytes 6291456 | tf_op jit(solution)/shard_map/half_product/pallas_call | solution.py:43
  4.6 8.8 %collective-permute-start = (f32[512,1024]{1,0:T(8,128)S(1)}, f32[512,1024]{1,0:T(8,128)S(1)}, u32[]{:S(2)}, u32[]{:S(2)}) collective-permute-start(f32[512,1024]{1,0:T(8,128)S(1)} %half_product.3), channel_id=1, source_target_pairs={{0,8},{8,0},{1,9},{9,1},{2,10},{10,2},{3,11},{11,3},{4,12},{12,4},... | collective-permute-start | bytes 6291464 | tf_op jit(solution)/shard_map/ppermute | solution.py:200
  13.4 0.0 copy-done.1
  13.4 1.8 %half_product.2 = f32[512,1024]{1,0:T(8,128)S(1)} custom-call(s32[1]{0:T(128)} %bitcast.half_ref, bf16[768,1024]{1,0:T(8,128)(2,1)S(1)} %copy-done.1, bf16[768,1024]{1,0:T(8,128)(2,1)S(1)} %copy-done.2), custom_call_target="tpu_custom_call" | custom-call | flops 805306368 | bytes 6291456 | tf_op jit(solution)/shard_map/half_product/pallas_call | solution.py:43
  15.2 2.0 %collective-permute-done = f32[512,1024]{1,0:T(8,128)S(1)} collective-permute-done((f32[512,1024]{1,0:T(8,128)S(1)}, f32[512,1024]{1,0:T(8,128)S(1)}, u32[]{:S(2)}, u32[]{:S(2)}) %collective-permute-start) | collective-permute-done | bytes 2097184 | tf_op jit(solution)/shard_map/ppermute | solution.py:200
  17.2 0.5 add.10
  17.6 43.6 %all_to_all.25 = f32[8,64,1024]{2,1,0:T(8,128)S(1)} all-to-all(f32[8,64,1024]{2,1,0:T(8,128)S(1)} %bitcast.8), channel_id=1, replica_groups={{0,16,32,48,64,80,96,112},{128,144,160,176,192,208,224,240},{256,272,28..., dimensions={0} | all-to-all | bytes 4194304 | tf_op jit(solution)/shard_map/all_to_all | solution.py:206
  61.2 0.1 reduce_sum.36
  61.3 14.9 %all_to_all.26 = f32[4,16,1024]{2,1,0:T(8,128)S(1)} all-to-all(f32[4,16,1024]{2,1,0:T(8,128)S(1)} %bitcast.9), channel_id=1, replica_groups={{0,128,256,384},{16,144,272,400},{32,160,288,416},{48,176,304,432},{64,..., dimensions={0} | all-to-all | bytes 524288 | tf_op jit(solution)/shard_map/all_to_all | solution.py:206
  76.3 9.6 %all_to_all.27 = bf16[4,16,1024]{2,1,0:T(8,128)(2,1)S(1)} all-to-all(bf16[4,16,1024]{2,1,0:T(8,128)(2,1)S(1)} %broadcast_in_dim.10), channel_id=1, replica_groups={{0,128,256,384},{16,144,272,400},{32,160,288,416},{48,176,304,432},{64,..., dimensions={0} | all-to-all | bytes 262144 | tf_op jit(solution)/shard_map/all_to_all | solution.py:211
  85.9 0.1 broadcast_in_dim.11
  86.0 24.8 %all_to_all.28 = bf16[8,64,1024]{2,1,0:T(8,128)(2,1)S(1)} all-to-all(bf16[8,64,1024]{2,1,0:T(8,128)(2,1)S(1)} %broadcast_in_dim.11), channel_id=1, replica_groups={{0,16,32,48,64,80,96,112},{128,144,160,176,192,208,224,240},{256,272,28..., dimensions={0} | all-to-all | bytes 2097152 | tf_op jit(solution)/shard_map/all_to_all | solution.py:211
  110.9 4.4 %collective-permute-start.1 = (bf16[512,1024]{1,0:T(8,128)(2,1)S(1)}, bf16[512,1024]{1,0:T(8,128)(2,1)S(1)}, u32[]{:S(2)}, u32[]{:S(2)}) collective-permute-start(bf16[512,1024]{1,0:T(8,128)(2,1)S(1)} %bitcast.6), channel_id=1, source_target_pairs={{0,8},{8,0},{1,9},{9,1},{2,10},{10,2},{3,11},{11,3},{4,12},{12,4},... | collective-permute-start | bytes 3145736 | tf_op jit(solution)/shard_map/ppermute | solution.py:213
  115.3 0.1 pad_add_fusion.place_ref
  115.4 2.2 %collective-permute-done.1.theirs_ref = bf16[512,1024]{1,0:T(8,128)(2,1)S(1)} collective-permute-done((bf16[512,1024]{1,0:T(8,128)(2,1)S(1)}, bf16[512,1024]{1,0:T(8,128)(2,1)S(1)}, u32[]{:S(2)}, u32[]{:S(2)}) %collective-permute-start.1) | collective-permute-done | bytes 1048608 | tf_op jit(solution)/shard_map/ppermute | solution.py:213
  117.6 41.4 %precondition.1 = (f32[16,1024]{1,0:T(8,128)S(1)}, f32[8,128]{1,0:T(8,128)S(1)}) custom-call(s32[2]{0:T(128)S(1)} %pad_add_fusion.place_ref, bf16[512,1024]{1,0:T(8,128)(2,1)S(1)} %bitcast.7, bf16[512,1024]{1,0:T(8,128)(2,1)S(1)} %collective-permute-done.1.theirs_ref), custom_call_target="tpu_custom_call" | custom-call | flops 25769803776 | bytes 3145728 | tf_op jit(solution)/shard_map/precondition/pallas_call | solution.py:175
  159.0 0.6 reduce_sum.38
  159.6 0.6 broadcast_in_dim.12
  160.3 10.0 %all_to_all.29 = f32[16,1,128]{2,1,0:T(1,128)S(1)} all-to-all(f32[16,1,128]{2,1,0:T(1,128)S(1)} %broadcast_in_dim.12), channel_id=1, replica_groups=mesh['z'=4,'y'=8,'c'=2,'group'=8] {'c','group'}, dimensions={0} | all-to-all | bytes 16384 | tf_op jit(solution)/shard_map/all_to_all | solution.py:218
  170.2 0.6 slice_reduce_fusion
  171.6 0.6 divide_convert_fusion
  (2 shorter events, 0.0 us)
Async XLA Ops:
  0.0 1.4 copy-start
  1.4 1.4 copy-start.2
  2.8 10.6 %copy-start.1 = (bf16[768,1024]{1,0:T(8,128)(2,1)S(1)}, bf16[768,1024]{1,0:T(8,128)(2,1)}, u32[]{:S(2)}) copy-start(bf16[768,1024]{1,0:T(8,128)(2,1)} %tokens_ref.3) | copy-start | bytes 4718596
  4.6 12.6 %collective-permute-start = (f32[512,1024]{1,0:T(8,128)S(1)}, f32[512,1024]{1,0:T(8,128)S(1)}, u32[]{:S(2)}, u32[]{:S(2)}) collective-permute-start(f32[512,1024]{1,0:T(8,128)S(1)} %half_product.3), channel_id=1, source_target_pairs={{0,8},{8,0},{1,9},{9,1},{2,10},{10,2},{3,11},{11,3},{4,12},{12,4},... | collective-permute-start | bytes 6291464 | tf_op jit(solution)/shard_map/ppermute | solution.py:200
  110.9 6.7 %collective-permute-start.1 = (bf16[512,1024]{1,0:T(8,128)(2,1)S(1)}, bf16[512,1024]{1,0:T(8,128)(2,1)S(1)}, u32[]{:S(2)}, u32[]{:S(2)}) collective-permute-start(bf16[512,1024]{1,0:T(8,128)(2,1)S(1)} %bitcast.6), channel_id=1, source_target_pairs={{0,8},{8,0},{1,9},{9,1},{2,10},{10,2},{3,11},{11,3},{4,12},{12,4},... | collective-permute-start | bytes 3145736 | tf_op jit(solution)/shard_map/ppermute | solution.py:213

commit v3 on v2

v3 whole, which is shorter than its diff:
```python
import jax
import jax.numpy as jnp
import numpy as np
from jax import lax
from jax.experimental import pallas as pl
from jax.experimental.pallas import tpu as pltpu
from jax.sharding import Mesh, PartitionSpec as P

Z, Y, C = 4, 8, 2
DP = ("z", "y", "c")
TILE = 256
VMEM = pl.BlockSpec(memory_space=pltpu.VMEM)
SMEM = pl.BlockSpec(memory_space=pltpu.SMEM)
f32, bf16 = jnp.float32, jnp.bfloat16


def device(z, y, c):
    return z * Y * C + y * C + c


Y_SETS = ((0, 2, 5, 7), (1, 3, 4, 6))
Z_SETS = ((0, 3), (1, 2))


def shifted(v, u, c):
    return device((v + c) % Z, (u + c) % Y, c)


def member(values, pair):
    return [v for v in values if v // 2 == pair][0]


FIRST = [
    [shifted(member(vs, m), member(us, p), c) for vs in Z_SETS for us in Y_SETS]
    for c in range(C)
    for m in range(Z // 2)
    for p in range(Y // 2)
]
SECOND = [
    [shifted(v, u, c) for v in vs for u in us] for c in range(C) for vs in Z_SETS for us in Y_SETS
]


def scalar(value):
    return jnp.full((1,), value, jnp.int32)


def normalise(precond, totals, elements):
    def body(precond_ref, totals_ref, out_ref):
        total = totals_ref[pl.ds(0, 8), :]
        for i in range(1, totals_ref.shape[0] // 8):
            total = total + totals_ref[pl.ds(8 * i, 8), :]
        scale = jnp.sqrt(total[0:1, 0:1] / elements + 1e-06)
        out_ref[...] = (precond_ref[...] / scale).astype(bf16)

    return pl.pallas_call(
        body,
        in_specs=[VMEM, VMEM],
        out_specs=VMEM,
        out_shape=jax.ShapeDtypeStruct(precond.shape, bf16),
        name="normalise",
    )(precond, totals)


def half_product(half, tokens, cotangent):
    depth, width = tokens.shape
    rows = width // C
    tiles, slabs = width // TILE, 3
    slab = depth // slabs

    def body(half_ref, tokens_ref, cotangent_ref, out_ref, held, turned, wide, sems, wide_sems):
        columns = pl.ds(pl.multiple_of(half_ref[0] * rows, rows), rows)
        copies = [
            pltpu.make_async_copy(
                tokens_ref.at[pl.ds(i * slab, slab), columns],
                held.at[pl.ds(i * slab, slab), :],
                sems.at[i],
            )
            for i in range(slabs)
        ] + [
            pltpu.make_async_copy(
                cotangent_ref.at[:, pl.ds(n * TILE, TILE)],
                wide.at[:, pl.ds(n * TILE, TILE)],
                wide_sems.at[n],
            )
            for n in range(tiles)
        ]
        for copy in copies:
            copy.start()
        for i in range(slabs):
            copies[i].wait()
            turned[:, pl.ds(i * slab, slab)] = held[pl.ds(i * slab, slab), :].T
        for n in range(tiles):
            copies[slabs + n].wait()
            here = pl.ds(n * TILE, TILE)
            out_ref[:, here] = jnp.dot(turned[...], wide[:, here], preferred_element_type=f32)

    return pl.pallas_call(
        body,
        in_specs=[SMEM, pl.BlockSpec(memory_space=pl.ANY), pl.BlockSpec(memory_space=pl.ANY)],
        out_specs=VMEM,
        out_shape=jax.ShapeDtypeStruct((rows, width), f32),
        scratch_shapes=[
            pltpu.VMEM((depth, rows), bf16),
            pltpu.VMEM((rows, depth), bf16),
            pltpu.VMEM((depth, width), bf16),
            pltpu.SemaphoreType.DMA((slabs,)),
            pltpu.SemaphoreType.DMA((tiles,)),
        ],
        compiler_params=pltpu.CompilerParams(vmem_limit_bytes=40 * 2**20),
        cost_estimate=pl.CostEstimate(
            flops=2 * depth * rows * width, bytes_accessed=6 * 2**20, transcendentals=0
        ),
        name="half_product",
    )(half, tokens, cotangent)


def precondition(place, mine, theirs, copies):
    half, width = mine.shape
    block = 16
    lo, hi = pl.ds(0, half), pl.ds(half, half)

    def body(place_ref, mine_ref, theirs_ref, rows_ref, square_ref, g, gt, sl, sr, xl, yl, xr, yr, f0l, f1l, f0r, f1r, h, k):
        core, own = place_ref[0], place_ref[1]
        g[pl.ds(pl.multiple_of(core * half, half), half), :] = mine_ref[...]
        g[pl.ds(pl.multiple_of((1 - core) * half, half), half), :] = theirs_ref[...]
        row = lax.broadcasted_iota(jnp.int32, (half, half), 0)
        column = lax.broadcasted_iota(jnp.int32, (half, half), 1)
        eye = row == column

        def dot(a, b):
            return jnp.dot(a, b, preferred_element_type=f32)

        def fold(square):
            return jnp.sum(square.reshape(-1, 8, square.shape[1]), axis=0)

        def factor(iterate, diagonal):
            if not diagonal:
                return (iterate * -0.25).astype(bf16)
            return (jnp.where(eye, 5.0 - iterate, -iterate) * 0.25).astype(bf16)

        def stat(a, b, out):
            s = dot(a[lo, :], b[:, lo])
            out[lo, lo] = s
            acc = fold(s * s)
            s = dot(a[lo, :], b[:, hi])
            out[lo, hi] = s
            acc = acc + 2.0 * fold(s * s)
            s = dot(a[hi, :], b[:, hi])
            out[hi, hi] = s
            acc = acc + fold(s * s)
            total = jnp.sum(jnp.sum(acc, axis=0, keepdims=True), axis=1, keepdims=True)
            return 1.0 / jnp.sqrt(total)

        def first(s, inverse, x, f):
            for r, c in ((lo, lo), (lo, hi), (hi, hi)):
                it = (s[r, c] * inverse).astype(bf16)
                x[r, c] = it
                fac = factor(it.astype(f32), r is c)
                f[r, c] = fac
                if r is not c:
                    x[c, r] = it.T
                    f[c, r] = fac.T

        def power(x, f, out):
            out[lo, lo] = dot(x[lo, :], f[:, lo]).astype(bf16)
            p = dot(x[...], f[:, hi]).astype(bf16)
            out[:, hi] = p
            out[hi, lo] = p[:half].T

        def last(x, f, out):
            it = dot(x[lo, :], f[:, lo]).astype(bf16)
            out[lo, lo] = factor(it.astype(f32), True)
            it = dot(x[...], f[:, hi]).astype(bf16).astype(f32)
            fac = factor(it[:half], False)
            out[lo, hi] = fac
            out[hi, lo] = fac.T
            out[hi, hi] = factor(it[half:], True)

        def times(x, f, out):
            for c in (lo, hi):
                out[:, c] = dot(x[...], f[:, c]).astype(bf16)

        gt[:, lo] = g[lo, :].T
        gt[:, hi] = g[hi, :].T
        inverse_l = stat(g, gt, sl)
        first(sl, inverse_l, xl, f0l)
        inverse_r = stat(gt, g, sr)
        power(xl, f0l, yl)
        first(sr, inverse_r, xr, f0r)
        power(yl, f0l, xl)
        power(xr, f0r, yr)
        power(xl, f0l, yl)
        power(yr, f0r, xr)
        last(yl, f0l, f1l)
        power(xr, f0r, yr)

        for i in range(half // block):
            source = pl.ds(pl.multiple_of((2 * i + core) * block, block), block)
            h[pl.ds(i * block, block), :] = f0l[source, :]
        times(h, f1l, k)
        last(yr, f0r, f1r)
        times(k, g, h)
        times(h, f0r, k)
        precond = sl
        acc = jnp.zeros((8, half), f32)
        for c in (lo, hi):
            p = dot(k[...], f1r[:, c])
            precond[lo, c] = p
            acc = acc + fold(p * p)
        total = jnp.sum(jnp.sum(acc, axis=0, keepdims=True), axis=1, keepdims=True)
        square_ref[...] = jnp.broadcast_to(total, square_ref.shape)
        rows_ref[...] = precond[pl.ds(pl.multiple_of(own * block, block), block), :]

    wide, stat_t = pltpu.VMEM((width, width), bf16), pltpu.VMEM((width, width), f32)
    narrow = pltpu.VMEM((half, width), bf16)
    return pl.pallas_call(
        body,
        in_specs=[SMEM, VMEM, VMEM],
        out_specs=[VMEM, VMEM],
        out_shape=[
            jax.ShapeDtypeStruct((block, width), f32),
            jax.ShapeDtypeStruct((8 * copies, 128), f32),
        ],
        scratch_shapes=[wide, wide, stat_t, stat_t] + [wide] * 8 + [narrow] * 2,
        compiler_params=pltpu.CompilerParams(vmem_limit_bytes=48 * 2**20),
        cost_estimate=pl.CostEstimate(
            flops=20 * width**3, bytes_accessed=3 * 2**20, transcendentals=0
        ),
        name="precondition",
    )(place, mine, theirs)


def on_device(tokens, cotangent):
    width = tokens.shape[1]
    z, y, c = lax.axis_index("z"), lax.axis_index("y"), lax.axis_index("c")
    core_swap = [(0, 1), (1, 0)]

    away = half_product(scalar(1 - c), tokens, cotangent)
    received = lax.ppermute(away, "c", core_swap)
    rows = half_product(scalar(c), tokens, cotangent) + received
    for groups in (FIRST, SECOND):
        count = len(groups[0])
        parts = rows.reshape(count, rows.shape[0] // count, width)
        rows = jnp.sum(lax.all_to_all(parts, DP, 0, 0, axis_index_groups=groups), axis=0)
    rows = rows.astype(bf16)
    for groups in (SECOND, FIRST):
        count = len(groups[0])
        copies = jnp.broadcast_to(rows, (count,) + rows.shape)
        rows = lax.all_to_all(copies, DP, 0, 0, axis_index_groups=groups)
        rows = rows.reshape(count * rows.shape[1], width)
    theirs = lax.ppermute(rows, "c", core_swap)

    groups = lax.axis_size("group")
    place = jnp.stack([c, z * Y + y]).astype(jnp.int32)
    precond, square = precondition(place, rows, theirs, C * groups)
    square = square.reshape(C * groups, 8, 128)
    totals = lax.all_to_all(square, ("c", "group"), 0, 0).reshape(C * groups * 8, 128)
    return normalise(precond, totals, groups * width * width)


def solution(mesh):
    groups = mesh.shape["group"]
    split = Mesh(np.asarray(mesh.devices).reshape(Z, Y, C, groups), DP + ("group",))
    return jax.shard_map(
        on_device,
        mesh=split,
        in_specs=(P(DP, None), P(DP, "group")),
        out_specs=P(DP, "group"),
        check_vma=False,
    )
```

time: 173 us -> 149 us (0.86)
  Pallas kernels: 45 us -> 29.8 us
  blocking collectives: 103 us -> 89.9 us
  starting transfers between devices: 13.2 us -> 21.2 us
  other arithmetic: 2.53 us -> 0.74 us
    pallas_call x1, Pallas kernels: 41.4 us -> 22.4 us  [precondition(): pl.pallas_call(body, in_specs=[SMEM, VMEM, VMEM], out_specs=[VMEM, VMEM],...]
    ppermute x1, starting transfers between devices: 4.43 us -> 12.4 us  [on_device(): theirs = lax.ppermute(rows, 'c', core_swap)]
    all_to_all x2, blocking collectives: 34.4 us -> 27.2 us  [on_device(): rows = lax.all_to_all(copies, DP, 0, 0, axis_index_groups=groups)]
    all_to_all x2, blocking collectives: 58.5 us -> 52.6 us  [on_device(): lax.all_to_all(parts, DP, 0, 0, axis_index_groups=groups)]
    pallas_call x2 -> x3, Pallas kernels: 3.6 us -> 7.4 us  [the longest x2 5.85 us: half_product(): pl.pallas_call(body, in_specs=[SMEM, pl.BlockSpec(memory_space=pl.ANY), p...]
  transfers between devices with their start and end apart: 2 -> 2, of which waited for: 2 -> 2; matrix products, arithmetic and copies ran while one was open for 0% -> 0% of each run, Pallas kernels for 1% -> 2%
where the time goes in v3:
time: 149 us; the launch traced here: 148 us
  blocking collectives  89.9 us (60%)
  Pallas kernels  29.8 us (20%)
  starting transfers between devices  21.2 us (14%)
  local copies, waits for them, and re-layouts  3.57 us (2%)
  waiting for transfers between devices  2.82 us (2%)
    all_to_all x2, blocking collectives, on_device(): lax.all_to_all(parts, DP, 0, 0, axis_index_groups=groups)  52.6 us
    all_to_all x2, blocking collectives, on_device(): rows = lax.all_to_all(copies, DP, 0, 0, axis_index_groups=groups)  27.2 us
    pallas_call x1, Pallas kernels, precondition(): pl.pallas_call(body, in_specs=[SMEM, VMEM, VMEM], out_specs=[VMEM, VMEM],...  22.4 us
    ppermute x1, starting transfers between devices, on_device(): theirs = lax.ppermute(rows, 'c', core_swap)  12.4 us
    all_to_all x1, blocking collectives, on_device(): lax.all_to_all(square, ('c', 'group'), 0, 0).reshape(C * groups * 8, 128)  10.1 us
    ppermute x1, starting transfers between devices, on_device(): received = lax.ppermute(away, 'c', core_swap)  8.79 us
    pallas_call x2, Pallas kernels, half_product(): pl.pallas_call(body, in_specs=[SMEM, pl.BlockSpec(memory_space=pl.ANY), p...  5.85 us
    unnamed x8, local copies, waits for them, and re-layouts  3.43 us
  transfers between devices with their start and end apart: 2, of which 2 were waited for; matrix products, arithmetic and copies ran while one was open for 0% of the time, Pallas kernels for 2%

profile of v3, /device:TPU:1, one launch (start us, length us, event | category | flops | bytes accessed | tf_op | source)
XLA Modules:
  0.0 148.2 jit_solution(11473924717733687893)
XLA Ops:
  0.0 0.0 copy-start
  0.0 1.4 copy-done
  1.4 0.0 copy-start.2
  1.4 1.4 copy-done.2
  2.8 0.0 copy-start.1
  2.8 2.9 %half_product.3 = f32[512,1024]{1,0:T(8,128)S(1)} custom-call(s32[1]{0:T(128)} %bitcast.2.half_ref, bf16[768,1024]{1,0:T(8,128)(2,1)S(1)} %copy-done, bf16[768,1024]{1,0:T(8,128)(2,1)S(1)} %copy-done.2), custom_call_target="tpu_custom_call" | custom-call | flops 805306368 | bytes 6291456 | tf_op jit(solution)/shard_map/half_product/pallas_call | solution.py:98
  5.7 8.8 %collective-permute-start = (f32[512,1024]{1,0:T(8,128)S(1)}, f32[512,1024]{1,0:T(8,128)S(1)}, u32[]{:S(2)}, u32[]{:S(2)}) collective-permute-start(f32[512,1024]{1,0:T(8,128)S(1)} %half_product.3), channel_id=1, source_target_pairs={{0,8},{8,0},{1,9},{9,1},{2,10},{10,2},{3,11},{11,3},{4,12},{12,4},... | collective-permute-start | bytes 6291464 | tf_op jit(solution)/shard_map/ppermute | solution.py:240
  14.5 0.0 copy-done.1
  14.5 2.9 %half_product.2 = f32[512,1024]{1,0:T(8,128)S(1)} custom-call(s32[1]{0:T(128)} %bitcast.half_ref, bf16[768,1024]{1,0:T(8,128)(2,1)S(1)} %copy-done.1, bf16[768,1024]{1,0:T(8,128)(2,1)S(1)} %copy-done.2), custom_call_target="tpu_custom_call" | custom-call | flops 805306368 | bytes 6291456 | tf_op jit(solution)/shard_map/half_product/pallas_call | solution.py:98
  17.5 0.8 collective-permute-done
  18.3 0.5 add.7
  18.8 34.4 %all_to_all.25 = f32[4,128,1024]{2,1,0:T(8,128)S(1)} all-to-all(f32[4,128,1024]{2,1,0:T(8,128)S(1)} %bitcast.12), channel_id=1, replica_groups={{0,16,128,144},{32,48,160,176},{80,64,208,192},{112,96,240,224},{384,40..., dimensions={0} | all-to-all | bytes 4194304 | tf_op jit(solution)/shard_map/all_to_all | solution.py:245
  53.2 0.2 reduce_sum.18
  53.4 18.2 %all_to_all.26 = f32[8,16,1024]{2,1,0:T(8,128)S(1)} all-to-all(f32[8,16,1024]{2,1,0:T(8,128)S(1)} %bitcast.13), channel_id=1, replica_groups={{0,32,80,112,384,416,464,496},{16,48,64,96,400,432,448,480},{128,160,20..., dimensions={0} | all-to-all | bytes 1048576 | tf_op jit(solution)/shard_map/all_to_all | solution.py:245
  71.6 10.4 %all_to_all.27 = bf16[8,16,1024]{2,1,0:T(8,128)(2,1)S(1)} all-to-all(bf16[8,16,1024]{2,1,0:T(8,128)(2,1)S(1)} %broadcast_in_dim.11), channel_id=1, replica_groups={{0,32,80,112,384,416,464,496},{16,48,64,96,400,432,448,480},{128,160,20..., dimensions={0} | all-to-all | bytes 524288 | tf_op jit(solution)/shard_map/all_to_all | solution.py:250
  82.1 0.1 broadcast_in_dim.12
  82.2 16.8 %all_to_all.28 = bf16[4,128,1024]{2,1,0:T(8,128)(2,1)S(1)} all-to-all(bf16[4,128,1024]{2,1,0:T(8,128)(2,1)S(1)} %broadcast_in_dim.12), channel_id=1, replica_groups={{0,16,128,144},{32,48,160,176},{80,64,208,192},{112,96,240,224},{384,40..., dimensions={0} | all-to-all | bytes 2097152 | tf_op jit(solution)/shard_map/all_to_all | solution.py:250
  98.9 12.4 %collective-permute-start.1 = (bf16[512,1024]{1,0:T(8,128)(2,1)S(1)}, bf16[512,1024]{1,0:T(8,128)(2,1)S(1)}, u32[]{:S(2)}, u32[]{:S(2)}) collective-permute-start(bf16[512,1024]{1,0:T(8,128)(2,1)S(1)} %bitcast.9), channel_id=1, source_target_pairs={{0,8},{8,0},{1,9},{9,1},{2,10},{10,2},{3,11},{11,3},{4,12},{12,4},... | collective-permute-start | bytes 3145736 | tf_op jit(solution)/shard_map/ppermute | solution.py:252
  111.4 0.1 pad_add_fusion.place_ref
  111.5 2.0 %collective-permute-done.1.theirs_ref = bf16[512,1024]{1,0:T(8,128)(2,1)S(1)} collective-permute-done((bf16[512,1024]{1,0:T(8,128)(2,1)S(1)}, bf16[512,1024]{1,0:T(8,128)(2,1)S(1)}, u32[]{:S(2)}, u32[]{:S(2)}) %collective-permute-start.1) | collective-permute-done | bytes 1048608 | tf_op jit(solution)/shard_map/ppermute | solution.py:252
  113.5 22.4 %precondition.1 = (f32[16,1024]{1,0:T(8,128)S(1)}, f32[128,128]{1,0:T(8,128)S(1)}) custom-call(s32[2]{0:T(128)S(1)} %pad_add_fusion.place_ref, bf16[512,1024]{1,0:T(8,128)(2,1)S(1)} %bitcast.10, bf16[512,1024]{1,0:T(8,128)(2,1)S(1)} %collective-permute-done.1.theirs_ref), custom_call_target="tpu_custom_call" | custom-call | flops 21474836480 | bytes 3145728 | tf_op jit(solution)/shard_map/precondition/pallas_call | solution.py:217
  135.9 0.0 copy-start.3
  135.9 0.6 copy-done.3
  136.5 10.1 %all_to_all.29 = f32[16,8,128]{2,1,0:T(8,128)} all-to-all(f32[16,8,128]{2,1,0:T(8,128)S(1)} %bitcast.11), channel_id=1, replica_groups=mesh['z'=4,'y'=8,'c'=2,'group'=8] {'c','group'}, dimensions={0} | all-to-all | bytes 131072 | tf_op jit(solution)/shard_map/all_to_all | solution.py:258
  146.6 1.6 %normalise.1 = bf16[16,1024]{1,0:T(8,128)(2,1)} custom-call(f32[16,1024]{1,0:T(8,128)} %copy-done.3, f32[128,128]{1,0:T(8,128)} %bitcast.15), custom_call_target="tpu_custom_call" | custom-call | tf_op jit(solution)/shard_map/normalise/pallas_call | solution.py:56
  (2 shorter events, 0.0 us)
Async XLA Ops:
  0.0 1.4 copy-start
  1.4 1.4 copy-start.2
  2.8 11.7 %copy-start.1 = (bf16[768,1024]{1,0:T(8,128)(2,1)S(1)}, bf16[768,1024]{1,0:T(8,128)(2,1)}, u32[]{:S(2)}) copy-start(bf16[768,1024]{1,0:T(8,128)(2,1)} %tokens_ref.3) | copy-start | bytes 4718596
  5.7 12.6 %collective-permute-start = (f32[512,1024]{1,0:T(8,128)S(1)}, f32[512,1024]{1,0:T(8,128)S(1)}, u32[]{:S(2)}, u32[]{:S(2)}) collective-permute-start(f32[512,1024]{1,0:T(8,128)S(1)} %half_product.3), channel_id=1, source_target_pairs={{0,8},{8,0},{1,9},{9,1},{2,10},{10,2},{3,11},{11,3},{4,12},{12,4},... | collective-permute-start | bytes 6291464 | tf_op jit(solution)/shard_map/ppermute | solution.py:240
  98.9 14.5 %collective-permute-start.1 = (bf16[512,1024]{1,0:T(8,128)(2,1)S(1)}, bf16[512,1024]{1,0:T(8,128)(2,1)S(1)}, u32[]{:S(2)}, u32[]{:S(2)}) collective-permute-start(bf16[512,1024]{1,0:T(8,128)(2,1)S(1)} %bitcast.9), channel_id=1, source_target_pairs={{0,8},{8,0},{1,9},{9,1},{2,10},{10,2},{3,11},{11,3},{4,12},{12,4},... | collective-permute-start | bytes 3145736 | tf_op jit(solution)/shard_map/ppermute | solution.py:252
  135.9 0.6 copy-start.3

commit v4 on v3

--- a/solution.py
+++ b/solution.py
@@ -11,6 +11,7 @@
 TILE = 256
 VMEM = pl.BlockSpec(memory_space=pltpu.VMEM)
 SMEM = pl.BlockSpec(memory_space=pltpu.SMEM)
+HBM = pl.BlockSpec(memory_space=pltpu.HBM)
 f32, bf16 = jnp.float32, jnp.bfloat16
 
 
@@ -58,17 +59,53 @@
         in_specs=[VMEM, VMEM],
         out_specs=VMEM,
         out_shape=jax.ShapeDtypeStruct(precond.shape, bf16),
+        compiler_params=pltpu.CompilerParams(vmem_limit_bytes=4 * 2**20),
         name="normalise",
     )(precond, totals)
 
 
 def half_product(half, tokens, cotangent):
+    depth, width = tokens.shape
+    rows = width // C
+
+    def body(half_ref, tokens_ref, cotangent_ref, out_ref, turned):
+        turned[...] = tokens_ref[...].T
+
+        @pl.loop(0, width // TILE)
+        def _(n):
+            columns = pl.ds(pl.multiple_of(n * TILE, TILE), TILE)
+            out_ref[:, columns] = jnp.dot(
+                turned[...], cotangent_ref[:, columns], preferred_element_type=f32
+            )
+
+    return pl.pallas_call(
+        body,
+        grid_spec=pltpu.PrefetchScalarGridSpec(
+            num_scalar_prefetch=1,
+            grid=(1,),
+            in_specs=[
+                pl.BlockSpec((depth, rows), lambda i, half: (0, half[0])),
+                pl.BlockSpec((depth, width), lambda i, half: (0, 0)),
+            ],
+            out_specs=pl.BlockSpec((rows, width), lambda i, half: (0, 0)),
+            scratch_shapes=[pltpu.VMEM((rows, depth), bf16)],
+        ),
+        out_shape=jax.ShapeDtypeStruct((rows, width), f32),
+        compiler_params=pltpu.CompilerParams(vmem_limit_bytes=40 * 2**20),
+        cost_estimate=pl.CostEstimate(
+            flops=2 * depth * rows * width, bytes_accessed=6 * 2**20, transcendentals=0
+        ),
+        name="half_product",
+    )(half, tokens, cotangent)
+
+
+def first_product(half, tokens, cotangent):
     depth, width = tokens.shape
     rows = width // C
     tiles, slabs = width // TILE, 3
     slab = depth // slabs
 
-    def body(half_ref, tokens_ref, cotangent_ref, out_ref, held, turned, wide, sems, wide_sems):
+    def body(half_ref, tokens_ref, cotangent_ref, out_ref, held, turned, wide, total, sems, wide_sems, out_sems):
         columns = pl.ds(pl.multiple_of(half_ref[0] * rows, rows), rows)
         copies = [
             pltpu.make_async_copy(
@@ -90,28 +127,37 @@
         for i in range(slabs):
             copies[i].wait()
             turned[:, pl.ds(i * slab, slab)] = held[pl.ds(i * slab, slab), :].T
+        out_copies = []
         for n in range(tiles):
             copies[slabs + n].wait()
             here = pl.ds(n * TILE, TILE)
-            out_ref[:, here] = jnp.dot(turned[...], wide[:, here], preferred_element_type=f32)
+            total[:, here] = jnp.dot(turned[...], wide[:, here], preferred_element_type=f32)
+            out_copies.append(
+                pltpu.make_async_copy(total.at[:, here], out_ref.at[:, here], out_sems.at[n])
+            )
+            out_copies[n].start()
+        for copy in out_copies:
+            copy.wait()
 
     return pl.pallas_call(
         body,
-        in_specs=[SMEM, pl.BlockSpec(memory_space=pl.ANY), pl.BlockSpec(memory_space=pl.ANY)],
-        out_specs=VMEM,
+        in_specs=[SMEM, HBM, HBM],
+        out_specs=HBM,
         out_shape=jax.ShapeDtypeStruct((rows, width), f32),
         scratch_shapes=[
             pltpu.VMEM((depth, rows), bf16),
             pltpu.VMEM((rows, depth), bf16),
             pltpu.VMEM((depth, width), bf16),
+            pltpu.VMEM((rows, width), f32),
             pltpu.SemaphoreType.DMA((slabs,)),
             pltpu.SemaphoreType.DMA((tiles,)),
+            pltpu.SemaphoreType.DMA((tiles,)),
         ],
-        compiler_params=pltpu.CompilerParams(vmem_limit_bytes=40 * 2**20),
+        compiler_params=pltpu.CompilerParams(vmem_limit_bytes=61_000_000),
         cost_estimate=pl.CostEstimate(
             flops=2 * depth * rows * width, bytes_accessed=6 * 2**20, transcendentals=0
         ),
-        name="half_product",
+        name="first_product",
     )(half, tokens, cotangent)
 
 
@@ -163,23 +209,14 @@
                     f[c, r] = fac.T
 
         def power(x, f, out):
-            out[lo, lo] = dot(x[lo, :], f[:, lo]).astype(bf16)
-            p = dot(x[...], f[:, hi]).astype(bf16)
-            out[:, hi] = p
-            out[hi, lo] = p[:half].T
-
-        def last(x, f, out):
-            it = dot(x[lo, :], f[:, lo]).astype(bf16)
-            out[lo, lo] = factor(it.astype(f32), True)
-            it = dot(x[...], f[:, hi]).astype(bf16).astype(f32)
-            fac = factor(it[:half], False)
-            out[lo, hi] = fac
-            out[hi, lo] = fac.T
-            out[hi, hi] = factor(it[half:], True)
-
-        def times(x, f, out):
             for c in (lo, hi):
                 out[:, c] = dot(x[...], f[:, c]).astype(bf16)
+
+        def last(x, f, out):
+            for c in (lo, hi):
+                it = dot(x[...], f[:, c]).astype(bf16).astype(f32)
+                out[lo, c] = factor(it[:half], c is lo)
+                out[hi, c] = factor(it[half:], c is hi)
 
         gt[:, lo] = g[lo, :].T
         gt[:, hi] = g[hi, :].T
@@ -198,10 +235,10 @@
         for i in range(half // block):
             source = pl.ds(pl.multiple_of((2 * i + core) * block, block), block)
             h[pl.ds(i * block, block), :] = f0l[source, :]
-        times(h, f1l, k)
+        power(h, f1l, k)
         last(yr, f0r, f1r)
-        times(k, g, h)
-        times(h, f0r, k)
+        power(k, g, h)
+        power(h, f0r, k)
         precond = sl
         acc = jnp.zeros((8, half), f32)
         for c in (lo, hi):
@@ -225,7 +262,7 @@
         scratch_shapes=[wide, wide, stat_t, stat_t] + [wide] * 8 + [narrow] * 2,
         compiler_params=pltpu.CompilerParams(vmem_limit_bytes=48 * 2**20),
         cost_estimate=pl.CostEstimate(
-            flops=20 * width**3, bytes_accessed=3 * 2**20, transcendentals=0
+            flops=23 * width**3, bytes_accessed=3 * 2**20, transcendentals=0
         ),
         name="precondition",
     )(place, mine, theirs)
@@ -236,7 +273,7 @@
     z, y, c = lax.axis_index("z"), lax.axis_index("y"), lax.axis_index("c")
     core_swap = [(0, 1), (1, 0)]
 
-    away = half_product(scalar(1 - c), tokens, cotangent)
+    away = first_product(scalar(1 - c), tokens, cotangent)
     received = lax.ppermute(away, "c", core_swap)
     rows = half_product(scalar(c), tokens, cotangent) + received
     for groups in (FIRST, SECOND):

time: 149 us -> 151 us (1.013)
  Pallas kernels: 29.8 us -> 34.1 us
  local copies, waits for them, and re-layouts: 3.57 us -> 0.14 us
    pallas_call x1, Pallas kernels: 22.4 us -> 26.6 us  [precondition(): pl.pallas_call(body, in_specs=[SMEM, VMEM, VMEM], out_specs=[VMEM, VMEM],...]
    unnamed x8 -> x4, local copies, waits for them, and re-layouts: 3.43 us -> 0.01 us
  transfers between devices with their start and end apart: 2 -> 2, of which waited for: 2 -> 2; matrix products, arithmetic and copies ran while one was open for 0% -> 0% of each run, Pallas kernels for 2% -> 1%
where the time goes in v4:
time: 151 us; the launch traced here: 150 us
  blocking collectives  89.8 us (59%)
  Pallas kernels  34.1 us (23%)
  starting transfers between devices  21.3 us (14%)
  waiting for transfers between devices  4.14 us (3%)
    all_to_all x2, blocking collectives, on_device(): lax.all_to_all(parts, DP, 0, 0, axis_index_groups=groups)  52.6 us
    all_to_all x2, blocking collectives, on_device(): rows = lax.all_to_all(copies, DP, 0, 0, axis_index_groups=groups)  27.1 us
    pallas_call x1, Pallas kernels, precondition(): pl.pallas_call(body, in_specs=[SMEM, VMEM, VMEM], out_specs=[VMEM, VMEM],...  26.6 us
    ppermute x1, starting transfers between devices, on_device(): theirs = lax.ppermute(rows, 'c', core_swap)  12.5 us
    all_to_all x1, blocking collectives, on_device(): lax.all_to_all(square, ('c', 'group'), 0, 0).reshape(C * groups * 8, 128)  10 us
    ppermute x1, starting transfers between devices, on_device(): received = lax.ppermute(away, 'c', core_swap)  8.79 us
    pallas_call x1, Pallas kernels, first_product(): pl.pallas_call(body, in_specs=[SMEM, HBM, HBM], out_specs=HBM, out_shape=...  4.94 us
  transfers between devices with their start and end apart: 2, of which 2 were waited for; matrix products, arithmetic and copies ran while one was open for 0% of the time, Pallas kernels for 1%

profile of v4, /device:TPU:1, one launch (start us, length us, event | category | flops | bytes accessed | tf_op | source)
XLA Modules:
  0.0 150.2 jit_solution(13669470094431606061)
XLA Ops:
  0.0 0.0 copy-start
  0.0 0.0 copy-start.1
  0.0 4.9 %first_product.1 = f32[512,1024]{1,0:T(8,128)} custom-call(s32[1]{0:T(128)} %bitcast.2.half_ref, bf16[768,1024]{1,0:T(8,128)(2,1)} %tokens_ref.3, bf16[768,1024]{1,0:T(8,128)(2,1)} %cotangent_ref.3), custom_call_target="tpu_custom_call" | custom-call | flops 805306368 | bytes 6291456 | tf_op jit(solution)/shard_map/first_product/pallas_call | solution.py:142
  5.0 8.8 %collective-permute-start = (f32[512,1024]{1,0:T(8,128)}, f32[512,1024]{1,0:T(8,128)S(1)}, u32[]{:S(2)}, u32[]{:S(2)}) collective-permute-start(f32[512,1024]{1,0:T(8,128)} %first_product.1), channel_id=1, source_target_pairs={{0,8},{8,0},{1,9},{9,1},{2,10},{10,2},{3,11},{11,3},{4,12},{12,4},... | collective-permute-start | bytes 6291464 | tf_op jit(solution)/shard_map/ppermute | solution.py:277
  13.7 0.0 copy-done
  13.8 0.0 copy-done.1
  13.8 1.8 %half_product.1 = f32[512,1024]{1,0:T(8,128)S(1)} custom-call(s32[1]{0:T(128)} %bitcast.half_ref, bf16[768,1024]{1,0:T(8,128)(2,1)S(1)} %copy-done, bf16[768,1024]{1,0:T(8,128)(2,1)S(1)} %copy-done.1), custom_call_target="tpu_custom_call" | custom-call | flops 805306368 | bytes 6291456 | tf_op jit(solution)/shard_map/half_product/pallas_call | solution.py:81
  15.6 2.1 %collective-permute-done = f32[512,1024]{1,0:T(8,128)S(1)} collective-permute-done((f32[512,1024]{1,0:T(8,128)}, f32[512,1024]{1,0:T(8,128)S(1)}, u32[]{:S(2)}, u32[]{:S(2)}) %collective-permute-start) | collective-permute-done | bytes 2097184 | tf_op jit(solution)/shard_map/ppermute | solution.py:277
  17.7 0.4 add.7
  18.1 34.4 %all_to_all.25 = f32[4,128,1024]{2,1,0:T(8,128)S(1)} all-to-all(f32[4,128,1024]{2,1,0:T(8,128)S(1)} %bitcast.13), channel_id=1, replica_groups={{0,16,128,144},{32,48,160,176},{80,64,208,192},{112,96,240,224},{384,40..., dimensions={0} | all-to-all | bytes 4194304 | tf_op jit(solution)/shard_map/all_to_all | solution.py:282
  52.5 0.2 reduce_sum.18
  52.7 18.2 %all_to_all.26 = f32[8,16,1024]{2,1,0:T(8,128)S(1)} all-to-all(f32[8,16,1024]{2,1,0:T(8,128)S(1)} %bitcast.14), channel_id=1, replica_groups={{0,32,80,112,384,416,464,496},{16,48,64,96,400,432,448,480},{128,160,20..., dimensions={0} | all-to-all | bytes 1048576 | tf_op jit(solution)/shard_map/all_to_all | solution.py:282
  71.0 10.4 %all_to_all.27 = bf16[8,16,1024]{2,1,0:T(8,128)(2,1)S(1)} all-to-all(bf16[8,16,1024]{2,1,0:T(8,128)(2,1)S(1)} %broadcast_in_dim.11), channel_id=1, replica_groups={{0,32,80,112,384,416,464,496},{16,48,64,96,400,432,448,480},{128,160,20..., dimensions={0} | all-to-all | bytes 524288 | tf_op jit(solution)/shard_map/all_to_all | solution.py:287
  81.4 0.1 broadcast_in_dim.12
  81.5 16.7 %all_to_all.28 = bf16[4,128,1024]{2,1,0:T(8,128)(2,1)S(1)} all-to-all(bf16[4,128,1024]{2,1,0:T(8,128)(2,1)S(1)} %broadcast_in_dim.12), channel_id=1, replica_groups={{0,16,128,144},{32,48,160,176},{80,64,208,192},{112,96,240,224},{384,40..., dimensions={0} | all-to-all | bytes 2097152 | tf_op jit(solution)/shard_map/all_to_all | solution.py:287
  98.3 12.5 %collective-permute-start.1 = (bf16[512,1024]{1,0:T(8,128)(2,1)S(1)}, bf16[512,1024]{1,0:T(8,128)(2,1)S(1)}, u32[]{:S(2)}, u32[]{:S(2)}) collective-permute-start(bf16[512,1024]{1,0:T(8,128)(2,1)S(1)} %bitcast.9), channel_id=1, source_target_pairs={{0,8},{8,0},{1,9},{9,1},{2,10},{10,2},{3,11},{11,3},{4,12},{12,4},... | collective-permute-start | bytes 3145736 | tf_op jit(solution)/shard_map/ppermute | solution.py:289
  110.8 0.1 pad_add_fusion.place_ref
  110.8 2.0 %collective-permute-done.1.theirs_ref = bf16[512,1024]{1,0:T(8,128)(2,1)S(1)} collective-permute-done((bf16[512,1024]{1,0:T(8,128)(2,1)S(1)}, bf16[512,1024]{1,0:T(8,128)(2,1)S(1)}, u32[]{:S(2)}, u32[]{:S(2)}) %collective-permute-start.1) | collective-permute-done | bytes 1048608 | tf_op jit(solution)/shard_map/ppermute | solution.py:289
  112.8 26.6 %precondition.1 = (f32[16,1024]{1,0:T(8,128)S(1)}, f32[128,128]{1,0:T(8,128)S(1)}) custom-call(s32[2]{0:T(128)S(1)} %pad_add_fusion.place_ref, bf16[512,1024]{1,0:T(8,128)(2,1)S(1)} %bitcast.10, bf16[512,1024]{1,0:T(8,128)(2,1)S(1)} %collective-permute-done.1.theirs_ref), custom_call_target="tpu_custom_call" | custom-call | flops 24696061952 | bytes 3145728 | tf_op jit(solution)/shard_map/precondition/pallas_call | solution.py:254
  139.5 10.0 %all_to_all.29 = f32[16,8,128]{2,1,0:T(8,128)S(1)} all-to-all(f32[16,8,128]{2,1,0:T(8,128)S(1)} %bitcast.12), channel_id=1, replica_groups=mesh['z'=4,'y'=8,'c'=2,'group'=8] {'c','group'}, dimensions={0} | all-to-all | bytes 131072 | tf_op jit(solution)/shard_map/all_to_all | solution.py:295
  149.5 0.7 normalise.1
  (2 shorter events, 0.0 us)
Async XLA Ops:
  0.0 13.7 %copy-start = (bf16[768,1024]{1,0:T(8,128)(2,1)S(1)}, bf16[768,1024]{1,0:T(8,128)(2,1)}, u32[]{:S(2)}) copy-start(bf16[768,1024]{1,0:T(8,128)(2,1)} %tokens_ref.3) | copy-start | bytes 4718596
  0.0 13.8 %copy-start.1 = (bf16[768,1024]{1,0:T(8,128)(2,1)S(1)}, bf16[768,1024]{1,0:T(8,128)(2,1)}, u32[]{:S(2)}) copy-start(bf16[768,1024]{1,0:T(8,128)(2,1)} %cotangent_ref.3) | copy-start | bytes 4718596
  5.0 12.8 %collective-permute-start = (f32[512,1024]{1,0:T(8,128)}, f32[512,1024]{1,0:T(8,128)S(1)}, u32[]{:S(2)}, u32[]{:S(2)}) collective-permute-start(f32[512,1024]{1,0:T(8,128)} %first_product.1), channel_id=1, source_target_pairs={{0,8},{8,0},{1,9},{9,1},{2,10},{10,2},{3,11},{11,3},{4,12},{12,4},... | collective-permute-start | bytes 6291464 | tf_op jit(solution)/shard_map/ppermute | solution.py:277
  98.3 14.6 %collective-permute-start.1 = (bf16[512,1024]{1,0:T(8,128)(2,1)S(1)}, bf16[512,1024]{1,0:T(8,128)(2,1)S(1)}, u32[]{:S(2)}, u32[]{:S(2)}) collective-permute-start(bf16[512,1024]{1,0:T(8,128)(2,1)S(1)} %bitcast.9), channel_id=1, source_target_pairs={{0,8},{8,0},{1,9},{9,1},{2,10},{10,2},{3,11},{11,3},{4,12},{12,4},... | collective-permute-start | bytes 3145736 | tf_op jit(solution)/shard_map/ppermute | solution.py:289

commit v5 on v4

--- a/solution.py
+++ b/solution.py
@@ -8,10 +8,9 @@
 
 Z, Y, C = 4, 8, 2
 DP = ("z", "y", "c")
-TILE = 256
+TILE = 512
 VMEM = pl.BlockSpec(memory_space=pltpu.VMEM)
 SMEM = pl.BlockSpec(memory_space=pltpu.SMEM)
-HBM = pl.BlockSpec(memory_space=pltpu.HBM)
 f32, bf16 = jnp.float32, jnp.bfloat16
 
 
@@ -71,9 +70,8 @@
     def body(half_ref, tokens_ref, cotangent_ref, out_ref, turned):
         turned[...] = tokens_ref[...].T
 
-        @pl.loop(0, width // TILE)
-        def _(n):
-            columns = pl.ds(pl.multiple_of(n * TILE, TILE), TILE)
+        for n in range(width // TILE):
+            columns = pl.ds(n * TILE, TILE)
             out_ref[:, columns] = jnp.dot(
                 turned[...], cotangent_ref[:, columns], preferred_element_type=f32
             )
@@ -99,104 +97,82 @@
     )(half, tokens, cotangent)
 
 
-def first_product(half, tokens, cotangent):
-    depth, width = tokens.shape
-    rows = width // C
-    tiles, slabs = width // TILE, 3
-    slab = depth // slabs
-
-    def body(half_ref, tokens_ref, cotangent_ref, out_ref, held, turned, wide, total, sems, wide_sems, out_sems):
-        columns = pl.ds(pl.multiple_of(half_ref[0] * rows, rows), rows)
-        copies = [
-            pltpu.make_async_copy(
-                tokens_ref.at[pl.ds(i * slab, slab), columns],
-                held.at[pl.ds(i * slab, slab), :],
-                sems.at[i],
-            )
-            for i in range(slabs)
-        ] + [
-            pltpu.make_async_copy(
-                cotangent_ref.at[:, pl.ds(n * TILE, TILE)],
-                wide.at[:, pl.ds(n * TILE, TILE)],
-                wide_sems.at[n],
-            )
-            for n in range(tiles)
-        ]
-        for copy in copies:
-            copy.start()
-        for i in range(slabs):
-            copies[i].wait()
-            turned[:, pl.ds(i * slab, slab)] = held[pl.ds(i * slab, slab), :].T
-        out_copies = []
-        for n in range(tiles):
-            copies[slabs + n].wait()
-            here = pl.ds(n * TILE, TILE)
-            total[:, here] = jnp.dot(turned[...], wide[:, here], preferred_element_type=f32)
-            out_copies.append(
-                pltpu.make_async_copy(total.at[:, here], out_ref.at[:, here], out_sems.at[n])
-            )
-            out_copies[n].start()
-        for copy in out_copies:
-            copy.wait()
-
-    return pl.pallas_call(
-        body,
-        in_specs=[SMEM, HBM, HBM],
-        out_specs=HBM,
-        out_shape=jax.ShapeDtypeStruct((rows, width), f32),
-        scratch_shapes=[
-            pltpu.VMEM((depth, rows), bf16),
-            pltpu.VMEM((rows, depth), bf16),
-            pltpu.VMEM((depth, width), bf16),
-            pltpu.VMEM((rows, width), f32),
-            pltpu.SemaphoreType.DMA((slabs,)),
-            pltpu.SemaphoreType.DMA((tiles,)),
-            pltpu.SemaphoreType.DMA((tiles,)),
+def dot(a, b):
+    return jnp.dot(a, b, preferred_element_type=f32)
+
+
+def fold(square):
+    return jnp.sum(square.reshape(-1, 8, square.shape[1]), axis=0)
+
+
+def own_share(mine):
+    half, width = mine.shape
+    lo, hi = pl.ds(0, half), pl.ds(half, half)
+
+    def body(mine_ref, turned_ref, right_ref, left_ref):
+        turned_ref[...] = mine_ref[...].T
+        left_ref[...] = dot(mine_ref[...], turned_ref[...])
+        right_ref[lo, lo] = dot(turned_ref[lo, :], mine_ref[:, lo])
+        right_ref[:, hi] = dot(turned_ref[...], mine_ref[:, hi])
+
+    return pl.pallas_call(
+        body,
+        in_specs=[VMEM],
+        out_specs=[VMEM, VMEM, VMEM],
+        out_shape=[
+            jax.ShapeDtypeStruct((width, half), bf16),
+            jax.ShapeDtypeStruct((width, width), f32),
+            jax.ShapeDtypeStruct((half, half), f32),
         ],
-        compiler_params=pltpu.CompilerParams(vmem_limit_bytes=61_000_000),
+        compiler_params=pltpu.CompilerParams(vmem_limit_bytes=24 * 2**20),
         cost_estimate=pl.CostEstimate(
-            flops=2 * depth * rows * width, bytes_accessed=6 * 2**20, transcendentals=0
-        ),
-        name="first_product",
-    )(half, tokens, cotangent)
-
-
-def precondition(place, mine, theirs, copies):
+            flops=2 * width**3, bytes_accessed=2**20, transcendentals=0
+        ),
+        name="own_share",
+    )(mine)
+
+
+def precondition(place, mine, theirs, turned, right, left, copies):
     half, width = mine.shape
     block = 16
     lo, hi = pl.ds(0, half), pl.ds(half, half)
 
-    def body(place_ref, mine_ref, theirs_ref, rows_ref, square_ref, g, gt, sl, sr, xl, yl, xr, yr, f0l, f1l, f0r, f1r, h, k):
+    def body(place_ref, mine_ref, theirs_ref, turned_ref, right_ref, left_ref, rows_ref, square_ref, g, gt, sl, sr, xl, yl, xr, yr, f0l, f1l, f0r, f1r, h, k, theirs_turned):
         core, own = place_ref[0], place_ref[1]
-        g[pl.ds(pl.multiple_of(core * half, half), half), :] = mine_ref[...]
-        g[pl.ds(pl.multiple_of((1 - core) * half, half), half), :] = theirs_ref[...]
+        ours = pl.ds(pl.multiple_of(core * half, half), half)
+        others = pl.ds(pl.multiple_of((1 - core) * half, half), half)
+        g[ours, :] = mine_ref[...]
+        g[others, :] = theirs_ref[...]
         row = lax.broadcasted_iota(jnp.int32, (half, half), 0)
         column = lax.broadcasted_iota(jnp.int32, (half, half), 1)
         eye = row == column
-
-        def dot(a, b):
-            return jnp.dot(a, b, preferred_element_type=f32)
-
-        def fold(square):
-            return jnp.sum(square.reshape(-1, 8, square.shape[1]), axis=0)
 
         def factor(iterate, diagonal):
             if not diagonal:
                 return (iterate * -0.25).astype(bf16)
             return (jnp.where(eye, 5.0 - iterate, -iterate) * 0.25).astype(bf16)
 
-        def stat(a, b, out):
-            s = dot(a[lo, :], b[:, lo])
-            out[lo, lo] = s
-            acc = fold(s * s)
-            s = dot(a[lo, :], b[:, hi])
-            out[lo, hi] = s
-            acc = acc + 2.0 * fold(s * s)
-            s = dot(a[hi, :], b[:, hi])
-            out[hi, hi] = s
-            acc = acc + fold(s * s)
+        def inverse_norm(diagonal, above):
+            acc = 2.0 * fold(above * above)
+            for s in diagonal:
+                acc = acc + fold(s * s)
             total = jnp.sum(jnp.sum(acc, axis=0, keepdims=True), axis=1, keepdims=True)
             return 1.0 / jnp.sqrt(total)
+
+        def left_stat():
+            s = dot(theirs_ref[...], theirs_turned[...])
+            sl[others, others] = s
+            sl[ours, ours] = left_ref[...]
+            above = dot(g[lo, :], gt[:, hi])
+            sl[lo, hi] = above
+            return inverse_norm([s, left_ref[...]], above)
+
+        def right_stat():
+            first_block = right_ref[lo, lo] + dot(theirs_turned[lo, :], theirs_ref[:, lo])
+            sr[lo, lo] = first_block
+            s = right_ref[:, hi] + dot(theirs_turned[...], theirs_ref[:, hi])
+            sr[:, hi] = s
+            return inverse_norm([first_block, s[half:]], s[:half])
 
         def first(s, inverse, x, f):
             for r, c in ((lo, lo), (lo, hi), (hi, hi)):
@@ -218,11 +194,12 @@
                 out[lo, c] = factor(it[:half], c is lo)
                 out[hi, c] = factor(it[half:], c is hi)
 
-        gt[:, lo] = g[lo, :].T
-        gt[:, hi] = g[hi, :].T
-        inverse_l = stat(g, gt, sl)
+        theirs_turned[...] = theirs_ref[...].T
+        gt[:, ours] = turned_ref[...]
+        gt[:, others] = theirs_turned[...]
+        inverse_l = left_stat()
         first(sl, inverse_l, xl, f0l)
-        inverse_r = stat(gt, g, sr)
+        inverse_r = right_stat()
         power(xl, f0l, yl)
         first(sr, inverse_r, xr, f0r)
         power(yl, f0l, xl)
@@ -253,19 +230,19 @@
     narrow = pltpu.VMEM((half, width), bf16)
     return pl.pallas_call(
         body,
-        in_specs=[SMEM, VMEM, VMEM],
+        in_specs=[SMEM] + [VMEM] * 5,
         out_specs=[VMEM, VMEM],
         out_shape=[
             jax.ShapeDtypeStruct((block, width), f32),
             jax.ShapeDtypeStruct((8 * copies, 128), f32),
         ],
-        scratch_shapes=[wide, wide, stat_t, stat_t] + [wide] * 8 + [narrow] * 2,
-        compiler_params=pltpu.CompilerParams(vmem_limit_bytes=48 * 2**20),
+        scratch_shapes=[wide, wide, stat_t, stat_t] + [wide] * 8 + [narrow] * 2 + [pltpu.VMEM((width, half), bf16)],
+        compiler_params=pltpu.CompilerParams(vmem_limit_bytes=44 * 2**20),
         cost_estimate=pl.CostEstimate(
             flops=23 * width**3, bytes_accessed=3 * 2**20, transcendentals=0
         ),
         name="precondition",
-    )(place, mine, theirs)
+    )(place, mine, theirs, turned, right, left)
 
 
 def on_device(tokens, cotangent):
@@ -273,7 +250,7 @@
     z, y, c = lax.axis_index("z"), lax.axis_index("y"), lax.axis_index("c")
     core_swap = [(0, 1), (1, 0)]
 
-    away = first_product(scalar(1 - c), tokens, cotangent)
+    away = half_product(scalar(1 - c), tokens, cotangent)
     received = lax.ppermute(away, "c", core_swap)
     rows = half_product(scalar(c), tokens, cotangent) + received
     for groups in (FIRST, SECOND):
@@ -290,7 +267,7 @@
 
     groups = lax.axis_size("group")
     place = jnp.stack([c, z * Y + y]).astype(jnp.int32)
-    precond, square = precondition(place, rows, theirs, C * groups)
+    precond, square = precondition(place, rows, theirs, *own_share(rows), C * groups)
     square = square.reshape(C * groups, 8, 128)
     totals = lax.all_to_all(square, ("c", "group"), 0, 0).reshape(C * groups * 8, 128)
     return normalise(precond, totals, groups * width * width)

time: 151 us -> 148 us (0.980)
  Pallas kernels: 34.1 us -> 29.5 us
  local copies, waits for them, and re-layouts: 0.14 us -> 2.95 us
    pallas_call x2, Pallas kernels: 31.6 us -> 26.7 us  [the longest x1 25.1 us: precondition(): pl.pallas_call(body, in_specs=[SMEM] + [VMEM] * 5, out_specs=[VMEM, VMEM]...]
    unnamed x4 -> x6, local copies, waits for them, and re-layouts: 0.01 us -> 2.82 us
    ppermute x1, waiting for transfers between devices: 2 us -> 0.39 us  [on_device(): theirs = lax.ppermute(rows, 'c', core_swap)]
  transfers between devices with their start and end apart: 2 -> 2, of which waited for: 2 -> 2; matrix products, arithmetic and copies ran while one was open for 0% -> 0% of each run, Pallas kernels for 1% -> 2%
where the time goes in v5:
time: 148 us; the launch traced here: 147 us
  blocking collectives  89.9 us (61%)
  Pallas kernels  29.5 us (20%)
  starting transfers between devices  21.2 us (14%)
  waiting for transfers between devices  3.11 us (2%)
  local copies, waits for them, and re-layouts  2.95 us (2%)
    all_to_all x2, blocking collectives, on_device(): lax.all_to_all(parts, DP, 0, 0, axis_index_groups=groups)  52.6 us
    all_to_all x2, blocking collectives, on_device(): rows = lax.all_to_all(copies, DP, 0, 0, axis_index_groups=groups)  27.2 us
    pallas_call x1, Pallas kernels, precondition(): pl.pallas_call(body, in_specs=[SMEM] + [VMEM] * 5, out_specs=[VMEM, VMEM]...  25.1 us
    ppermute x1, starting transfers between devices, on_device(): theirs = lax.ppermute(rows, 'c', core_swap)  12.4 us
    all_to_all x1, blocking collectives, on_device(): lax.all_to_all(square, ('c', 'group'), 0, 0).reshape(C * groups * 8, 128)  10.1 us
    ppermute x1, starting transfers between devices, on_device(): received = lax.ppermute(away, 'c', core_swap)  8.79 us
  transfers between devices with their start and end apart: 2, of which 2 were waited for; matrix products, arithmetic and copies ran while one was open for 0% of the time, Pallas kernels for 2%

profile of v5, /device:TPU:1, one launch (start us, length us, event | category | flops | bytes accessed | tf_op | source)
XLA Modules:
  0.0 147.5 jit_solution(14982481152395975463)
XLA Ops:
  0.0 0.0 copy-start
  0.0 1.4 copy-done
  1.4 0.0 copy-start.2
  1.4 1.4 copy-done.2
  2.8 0.0 copy-start.1
  2.8 1.0 half_product.3
  3.8 8.8 %collective-permute-start = (f32[512,1024]{1,0:T(8,128)S(1)}, f32[512,1024]{1,0:T(8,128)S(1)}, u32[]{:S(2)}, u32[]{:S(2)}) collective-permute-start(f32[512,1024]{1,0:T(8,128)S(1)} %half_product.3), channel_id=1, source_target_pairs={{0,8},{8,0},{1,9},{9,1},{2,10},{10,2},{3,11},{11,3},{4,12},{12,4},... | collective-permute-start | bytes 6291464 | tf_op jit(solution)/shard_map/ppermute | solution.py:254
  12.6 0.0 copy-done.1
  12.6 1.0 half_product.2
  13.7 2.7 %collective-permute-done = f32[512,1024]{1,0:T(8,128)S(1)} collective-permute-done((f32[512,1024]{1,0:T(8,128)S(1)}, f32[512,1024]{1,0:T(8,128)S(1)}, u32[]{:S(2)}, u32[]{:S(2)}) %collective-permute-start) | collective-permute-done | bytes 2097184 | tf_op jit(solution)/shard_map/ppermute | solution.py:254
  16.4 0.5 add.7
  16.9 34.4 %all_to_all.25 = f32[4,128,1024]{2,1,0:T(8,128)S(1)} all-to-all(f32[4,128,1024]{2,1,0:T(8,128)S(1)} %bitcast.14), channel_id=1, replica_groups={{0,16,128,144},{32,48,160,176},{80,64,208,192},{112,96,240,224},{384,40..., dimensions={0} | all-to-all | bytes 4194304 | tf_op jit(solution)/shard_map/all_to_all | solution.py:259
  51.3 0.2 reduce_sum.18
  51.5 18.2 %all_to_all.26 = f32[8,16,1024]{2,1,0:T(8,128)S(1)} all-to-all(f32[8,16,1024]{2,1,0:T(8,128)S(1)} %bitcast.15), channel_id=1, replica_groups={{0,32,80,112,384,416,464,496},{16,48,64,96,400,432,448,480},{128,160,20..., dimensions={0} | all-to-all | bytes 1048576 | tf_op jit(solution)/shard_map/all_to_all | solution.py:259
  69.7 10.4 %all_to_all.27 = bf16[8,16,1024]{2,1,0:T(8,128)(2,1)S(1)} all-to-all(bf16[8,16,1024]{2,1,0:T(8,128)(2,1)S(1)} %broadcast_in_dim.11), channel_id=1, replica_groups={{0,32,80,112,384,416,464,496},{16,48,64,96,400,432,448,480},{128,160,20..., dimensions={0} | all-to-all | bytes 524288 | tf_op jit(solution)/shard_map/all_to_all | solution.py:264
  80.2 0.1 broadcast_in_dim.12
  80.3 16.8 %all_to_all.28 = bf16[4,128,1024]{2,1,0:T(8,128)(2,1)S(1)} all-to-all(bf16[4,128,1024]{2,1,0:T(8,128)(2,1)S(1)} %broadcast_in_dim.12), channel_id=1, replica_groups={{0,16,128,144},{32,48,160,176},{80,64,208,192},{112,96,240,224},{384,40..., dimensions={0} | all-to-all | bytes 2097152 | tf_op jit(solution)/shard_map/all_to_all | solution.py:264
  97.0 12.4 %collective-permute-start.1 = (bf16[512,1024]{1,0:T(8,128)(2,1)S(1)}, bf16[512,1024]{1,0:T(8,128)(2,1)S(1)}, u32[]{:S(2)}, u32[]{:S(2)}) collective-permute-start(bf16[512,1024]{1,0:T(8,128)(2,1)S(1)} %bitcast.9), channel_id=1, source_target_pairs={{0,8},{8,0},{1,9},{9,1},{2,10},{10,2},{3,11},{11,3},{4,12},{12,4},... | collective-permute-start | bytes 3145736 | tf_op jit(solution)/shard_map/ppermute | solution.py:266
  109.5 0.1 pad_add_fusion.place_ref
  109.6 1.6 %own_share.1 = (bf16[1024,512]{1,0:T(8,128)(2,1)S(1)}, f32[1024,1024]{1,0:T(8,128)S(1)}, f32[512,512]{1,0:T(8,128)S(1)}) custom-call(bf16[512,1024]{1,0:T(8,128)(2,1)S(1)} %bitcast.10), custom_call_target="tpu_custom_call" | custom-call | flops 2147483648 | bytes 1048576 | tf_op jit(solution)/shard_map/own_share/pallas_call | solution.py:118
  111.2 0.4 collective-permute-done.1.theirs_ref
  111.6 25.1 %precondition.1 = (f32[16,1024]{1,0:T(8,128)S(1)}, f32[128,128]{1,0:T(8,128)S(1)}) custom-call(s32[2]{0:T(128)S(1)} %pad_add_fusion.place_ref, bf16[512,1024]{1,0:T(8,128)(2,1)S(1)} %bitcast.11, bf16[512,1024]{1,0:T(8,128)(2,1)S(1)} %collective-permute-done.1.theirs_ref, bf16[1024,512]{1,0:T(8,128)(2,1)S(1)} %get-tuple-element.10.turned_ref, ...), custom_call_target="tpu_custom_call" | custom-call | flops 24696061952 | bytes 3145728 | tf_op jit(solution)/shard_map/precondition/pallas_call | solution.py:231
  136.7 10.1 %all_to_all.29 = f32[16,8,128]{2,1,0:T(8,128)S(1)} all-to-all(f32[16,8,128]{2,1,0:T(8,128)S(1)} %bitcast.13), channel_id=1, replica_groups=mesh['z'=4,'y'=8,'c'=2,'group'=8] {'c','group'}, dimensions={0} | all-to-all | bytes 131072 | tf_op jit(solution)/shard_map/all_to_all | solution.py:272
  146.8 0.7 normalise.1
  (2 shorter events, 0.0 us)
Async XLA Ops:
  0.0 1.4 copy-start
  1.4 1.4 copy-start.2
  2.8 9.8 %copy-start.1 = (bf16[768,1024]{1,0:T(8,128)(2,1)S(1)}, bf16[768,1024]{1,0:T(8,128)(2,1)}, u32[]{:S(2)}) copy-start(bf16[768,1024]{1,0:T(8,128)(2,1)} %tokens_ref.3) | copy-start | bytes 4718596
  3.8 12.6 %collective-permute-start = (f32[512,1024]{1,0:T(8,128)S(1)}, f32[512,1024]{1,0:T(8,128)S(1)}, u32[]{:S(2)}, u32[]{:S(2)}) collective-permute-start(f32[512,1024]{1,0:T(8,128)S(1)} %half_product.3), channel_id=1, source_target_pairs={{0,8},{8,0},{1,9},{9,1},{2,10},{10,2},{3,11},{11,3},{4,12},{12,4},... | collective-permute-start | bytes 6291464 | tf_op jit(solution)/shard_map/ppermute | solution.py:254
  97.0 14.5 %collective-permute-start.1 = (bf16[512,1024]{1,0:T(8,128)(2,1)S(1)}, bf16[512,1024]{1,0:T(8,128)(2,1)S(1)}, u32[]{:S(2)}, u32[]{:S(2)}) collective-permute-start(bf16[512,1024]{1,0:T(8,128)(2,1)S(1)} %bitcast.9), channel_id=1, source_target_pairs={{0,8},{8,0},{1,9},{9,1},{2,10},{10,2},{3,11},{11,3},{4,12},{12,4},... | collective-permute-start | bytes 3145736 | tf_op jit(solution)/shard_map/ppermute | solution.py:266

commit v6 on v5

--- a/solution.py
+++ b/solution.py
@@ -188,8 +188,8 @@
             for c in (lo, hi):
                 out[:, c] = dot(x[...], f[:, c]).astype(bf16)
 
-        def last(x, f, out):
-            for c in (lo, hi):
+        def last(x, f, out, columns):
+            for c in columns:
                 it = dot(x[...], f[:, c]).astype(bf16).astype(f32)
                 out[lo, c] = factor(it[:half], c is lo)
                 out[hi, c] = factor(it[half:], c is hi)
@@ -205,16 +205,16 @@
         power(yl, f0l, xl)
         power(xr, f0r, yr)
         power(xl, f0l, yl)
-        power(yr, f0r, xr)
-        last(yl, f0l, f1l)
-        power(xr, f0r, yr)
-
         for i in range(half // block):
             source = pl.ds(pl.multiple_of((2 * i + core) * block, block), block)
             h[pl.ds(i * block, block), :] = f0l[source, :]
+        power(yr, f0r, xr)
+        last(yl, f0l, f1l, (lo, hi))
+        power(xr, f0r, yr)
         power(h, f1l, k)
-        last(yr, f0r, f1r)
+        last(yr, f0r, f1r, (lo,))
         power(k, g, h)
+        last(yr, f0r, f1r, (hi,))
         power(h, f0r, k)
         precond = sl
         acc = jnp.zeros((8, half), f32)
@@ -247,6 +247,7 @@
 
 def on_device(tokens, cotangent):
     width = tokens.shape[1]
+    half = width // C
     z, y, c = lax.axis_index("z"), lax.axis_index("y"), lax.axis_index("c")
     core_swap = [(0, 1), (1, 0)]
 
@@ -258,11 +259,9 @@
         parts = rows.reshape(count, rows.shape[0] // count, width)
         rows = jnp.sum(lax.all_to_all(parts, DP, 0, 0, axis_index_groups=groups), axis=0)
     rows = rows.astype(bf16)
-    for groups in (SECOND, FIRST):
-        count = len(groups[0])
-        copies = jnp.broadcast_to(rows, (count,) + rows.shape)
-        rows = lax.all_to_all(copies, DP, 0, 0, axis_index_groups=groups)
-        rows = rows.reshape(count * rows.shape[1], width)
+    rows = lax.all_gather(rows, DP, axis_index_groups=SECOND, axis=0, tiled=True)
+    copies = jnp.broadcast_to(rows, (len(FIRST[0]),) + rows.shape)
+    rows = lax.all_to_all(copies, DP, 0, 0, axis_index_groups=FIRST).reshape(half, width)
     theirs = lax.ppermute(rows, "c", core_swap)
 
     groups = lax.axis_size("group")

time: 148 us -> 178 us (1.20)
  blocking collectives: 89.9 us -> 113 us
  starting transfers between devices: 21.2 us -> 28.2 us
    all_gather x0 -> x1, blocking collectives: none -> 25.3 us  [on_device(): lax.all_gather(rows, DP, axis_index_groups=SECOND, axis=0, tiled=True)]
    ppermute x1, starting transfers between devices: 12.4 us -> 19.5 us  [on_device(): theirs = lax.ppermute(rows, 'c', core_swap)]
    all_to_all x2 -> x1, blocking collectives: 27.2 us -> 24.6 us  [on_device(): lax.all_to_all(copies, DP, 0, 0, axis_index_groups=FIRST)]
  transfers between devices with their start and end apart: 2 -> 2, of which waited for: 2 -> 2; matrix products, arithmetic and copies ran while one was open for 0% -> 0% of each run, Pallas kernels for 2% -> 1%
where the time goes in v6:
time: 178 us; the launch traced here: 177 us
  blocking collectives  113 us (63%)
  Pallas kernels  29.5 us (17%)
  starting transfers between devices  28.2 us (16%)
  waiting for transfers between devices  3.11 us (2%)
  local copies, waits for them, and re-layouts  2.94 us (2%)
    all_to_all x2, blocking collectives, on_device(): lax.all_to_all(parts, DP, 0, 0, axis_index_groups=groups)  52.6 us
    all_gather x1, blocking collectives, on_device(): lax.all_gather(rows, DP, axis_index_groups=SECOND, axis=0, tiled=True)  25.3 us
    pallas_call x1, Pallas kernels, precondition(): pl.pallas_call(body, in_specs=[SMEM] + [VMEM] * 5, out_specs=[VMEM, VMEM]...  25.1 us
    all_to_all x1, blocking collectives, on_device(): lax.all_to_all(copies, DP, 0, 0, axis_index_groups=FIRST)  24.6 us
    ppermute x1, starting transfers between devices, on_device(): theirs = lax.ppermute(rows, 'c', core_swap)  19.5 us
    all_to_all x1, blocking collectives, on_device(): lax.all_to_all(square, ('c', 'group'), 0, 0).reshape(C * groups * 8, 128)  10.3 us
    ppermute x1, starting transfers between devices, on_device(): received = lax.ppermute(away, 'c', core_swap)  8.79 us
  transfers between devices with their start and end apart: 2, of which 2 were waited for; matrix products, arithmetic and copies ran while one was open for 0% of the time, Pallas kernels for 1%

profile of v6, /device:TPU:1, one launch (start us, length us, event | category | flops | bytes accessed | tf_op | source)
XLA Modules:
  0.0 177.4 jit_solution(10695616068542261267)
XLA Ops:
  0.0 0.0 copy-start
  0.0 1.4 copy-done
  1.4 0.0 copy-start.2
  1.4 1.4 copy-done.2
  2.8 0.0 copy-start.1
  2.8 1.0 half_product.3
  3.8 8.8 %collective-permute-start = (f32[512,1024]{1,0:T(8,128)S(1)}, f32[512,1024]{1,0:T(8,128)S(1)}, u32[]{:S(2)}, u32[]{:S(2)}) collective-permute-start(f32[512,1024]{1,0:T(8,128)S(1)} %half_product.3), channel_id=1, source_target_pairs={{0,8},{8,0},{1,9},{9,1},{2,10},{10,2},{3,11},{11,3},{4,12},{12,4},... | collective-permute-start | bytes 6291464 | tf_op jit(solution)/shard_map/ppermute | solution.py:255
  12.6 0.0 copy-done.1
  12.6 1.0 half_product.2
  13.7 2.7 %collective-permute-done = f32[512,1024]{1,0:T(8,128)S(1)} collective-permute-done((f32[512,1024]{1,0:T(8,128)S(1)}, f32[512,1024]{1,0:T(8,128)S(1)}, u32[]{:S(2)}, u32[]{:S(2)}) %collective-permute-start) | collective-permute-done | bytes 2097184 | tf_op jit(solution)/shard_map/ppermute | solution.py:255
  16.4 0.5 add.7
  16.9 34.4 %all_to_all.20 = f32[4,128,1024]{2,1,0:T(8,128)S(1)} all-to-all(f32[4,128,1024]{2,1,0:T(8,128)S(1)} %bitcast.13), channel_id=1, replica_groups={{0,16,128,144},{32,48,160,176},{80,64,208,192},{112,96,240,224},{384,40..., dimensions={0} | all-to-all | bytes 4194304 | tf_op jit(solution)/shard_map/all_to_all | solution.py:260
  51.3 0.2 reduce_sum.18
  51.5 18.2 %all_to_all.21 = f32[8,16,1024]{2,1,0:T(8,128)S(1)} all-to-all(f32[8,16,1024]{2,1,0:T(8,128)S(1)} %bitcast.14), channel_id=1, replica_groups={{0,32,80,112,384,416,464,496},{16,48,64,96,400,432,448,480},{128,160,20..., dimensions={0} | all-to-all | bytes 1048576 | tf_op jit(solution)/shard_map/all_to_all | solution.py:260
  69.7 25.3 %all_gather.3 = bf16[128,1024]{1,0:T(8,128)(2,1)S(1)} all-gather(bf16[16,1024]{1,0:T(8,128)(2,1)S(1)} %reduce_sum.19), channel_id=1, replica_groups={{0,32,80,112,384,416,464,496},{16,48,64,96,400,432,448,480},{128,160,20..., dimensions={0}, use_global_device_ids=true | all-gather | bytes 294912 | tf_op jit(solution)/shard_map/all_gather | solution.py:262
  95.0 0.1 broadcast_in_dim.8
  95.2 24.6 %all_to_all.22 = bf16[4,128,1024]{2,1,0:T(8,128)(2,1)S(1)} all-to-all(bf16[4,128,1024]{2,1,0:T(8,128)(2,1)S(1)} %broadcast_in_dim.8), channel_id=1, replica_groups={{0,16,128,144},{32,48,160,176},{80,64,208,192},{112,96,240,224},{384,40..., dimensions={0} | all-to-all | bytes 2097152 | tf_op jit(solution)/shard_map/all_to_all | solution.py:264
  119.8 19.5 %collective-permute-start.1 = (bf16[512,1024]{1,0:T(8,128)(2,1)S(1)}, bf16[512,1024]{1,0:T(8,128)(2,1)S(1)}, u32[]{:S(2)}, u32[]{:S(2)}) collective-permute-start(bf16[512,1024]{1,0:T(8,128)(2,1)S(1)} %bitcast.8), channel_id=1, source_target_pairs={{0,8},{8,0},{1,9},{9,1},{2,10},{10,2},{3,11},{11,3},{4,12},{12,4},... | collective-permute-start | bytes 3145736 | tf_op jit(solution)/shard_map/ppermute | solution.py:265
  139.3 0.1 pad_add_fusion.place_ref
  139.3 1.6 own_share.1
  140.9 0.4 collective-permute-done.1.theirs_ref
  141.3 25.1 %precondition.1 = (f32[16,1024]{1,0:T(8,128)S(1)}, f32[128,128]{1,0:T(8,128)S(1)}) custom-call(s32[2]{0:T(128)S(1)} %pad_add_fusion.place_ref, bf16[512,1024]{1,0:T(8,128)(2,1)S(1)} %bitcast.10, bf16[512,1024]{1,0:T(8,128)(2,1)S(1)} %collective-permute-done.1.theirs_ref, bf16[1024,512]{1,0:T(8,128)(2,1)S(1)} %get-tuple-element.10.turned_ref, ...), custom_call_target="tpu_custom_call" | custom-call | flops 24696061952 | bytes 3145728 | tf_op jit(solution)/shard_map/precondition/pallas_call | solution.py:231
  166.5 10.3 %all_to_all.23 = f32[16,8,128]{2,1,0:T(8,128)S(1)} all-to-all(f32[16,8,128]{2,1,0:T(8,128)S(1)} %bitcast.12), channel_id=1, replica_groups=mesh['z'=4,'y'=8,'c'=2,'group'=8] {'c','group'}, dimensions={0} | all-to-all | bytes 131072 | tf_op jit(solution)/shard_map/all_to_all | solution.py:271
  176.7 0.7 normalise.1
  (1 shorter events, 0.0 us)
Async XLA Ops:
  0.0 1.4 copy-start
  1.4 1.4 copy-start.2
  2.8 9.8 %copy-start.1 = (bf16[768,1024]{1,0:T(8,128)(2,1)S(1)}, bf16[768,1024]{1,0:T(8,128)(2,1)}, u32[]{:S(2)}) copy-start(bf16[768,1024]{1,0:T(8,128)(2,1)} %tokens_ref.3) | copy-start | bytes 4718596
  3.8 12.6 %collective-permute-start = (f32[512,1024]{1,0:T(8,128)S(1)}, f32[512,1024]{1,0:T(8,128)S(1)}, u32[]{:S(2)}, u32[]{:S(2)}) collective-permute-start(f32[512,1024]{1,0:T(8,128)S(1)} %half_product.3), channel_id=1, source_target_pairs={{0,8},{8,0},{1,9},{9,1},{2,10},{10,2},{3,11},{11,3},{4,12},{12,4},... | collective-permute-start | bytes 6291464 | tf_op jit(solution)/shard_map/ppermute | solution.py:255
  119.8 21.5 %collective-permute-start.1 = (bf16[512,1024]{1,0:T(8,128)(2,1)S(1)}, bf16[512,1024]{1,0:T(8,128)(2,1)S(1)}, u32[]{:S(2)}, u32[]{:S(2)}) collective-permute-start(bf16[512,1024]{1,0:T(8,128)(2,1)S(1)} %bitcast.8), channel_id=1, source_target_pairs={{0,8},{8,0},{1,9},{9,1},{2,10},{10,2},{3,11},{11,3},{4,12},{12,4},... | collective-permute-start | bytes 3145736 | tf_op jit(solution)/shard_map/ppermute | solution.py:265

commit v7 on v5

--- a/solution.py
+++ b/solution.py
@@ -95,6 +95,32 @@
         ),
         name="half_product",
     )(half, tokens, cotangent)
+
+
+def product(tokens, cotangent):
+    depth, rows = tokens.shape
+    width = cotangent.shape[1]
+
+    def body(tokens_ref, cotangent_ref, out_ref, turned):
+        turned[...] = tokens_ref[...].T
+        for n in range(width // TILE):
+            columns = pl.ds(n * TILE, TILE)
+            out_ref[:, columns] = jnp.dot(
+                turned[...], cotangent_ref[:, columns], preferred_element_type=f32
+            )
+
+    return pl.pallas_call(
+        body,
+        in_specs=[VMEM] * 2,
+        out_specs=VMEM,
+        out_shape=jax.ShapeDtypeStruct((rows, width), f32),
+        scratch_shapes=[pltpu.VMEM((rows, depth), bf16)],
+        compiler_params=pltpu.CompilerParams(vmem_limit_bytes=40 * 2**20),
+        cost_estimate=pl.CostEstimate(
+            flops=2 * depth * rows * width, bytes_accessed=6 * 2**20, transcendentals=0
+        ),
+        name="product",
+    )(tokens, cotangent)
 
 
 def dot(a, b):
@@ -152,12 +178,12 @@
                 return (iterate * -0.25).astype(bf16)
             return (jnp.where(eye, 5.0 - iterate, -iterate) * 0.25).astype(bf16)
 
-        def inverse_norm(diagonal, above):
+        def norm(diagonal, above):
             acc = 2.0 * fold(above * above)
             for s in diagonal:
                 acc = acc + fold(s * s)
             total = jnp.sum(jnp.sum(acc, axis=0, keepdims=True), axis=1, keepdims=True)
-            return 1.0 / jnp.sqrt(total)
+            return jnp.sqrt(total)
 
         def left_stat():
             s = dot(theirs_ref[...], theirs_turned[...])
@@ -165,18 +191,18 @@
             sl[ours, ours] = left_ref[...]
             above = dot(g[lo, :], gt[:, hi])
             sl[lo, hi] = above
-            return inverse_norm([s, left_ref[...]], above)
+            return norm([s, left_ref[...]], above)
 
         def right_stat():
             first_block = right_ref[lo, lo] + dot(theirs_turned[lo, :], theirs_ref[:, lo])
             sr[lo, lo] = first_block
             s = right_ref[:, hi] + dot(theirs_turned[...], theirs_ref[:, hi])
             sr[:, hi] = s
-            return inverse_norm([first_block, s[half:]], s[:half])
-
-        def first(s, inverse, x, f):
+            return norm([first_block, s[half:]], s[:half])
+
+        def first(s, size, x, f):
             for r, c in ((lo, lo), (lo, hi), (hi, hi)):
-                it = (s[r, c] * inverse).astype(bf16)
+                it = (s[r, c] / size).astype(bf16)
                 x[r, c] = it
                 fac = factor(it.astype(f32), r is c)
                 f[r, c] = fac
@@ -197,11 +223,11 @@
         theirs_turned[...] = theirs_ref[...].T
         gt[:, ours] = turned_ref[...]
         gt[:, others] = theirs_turned[...]
-        inverse_l = left_stat()
-        first(sl, inverse_l, xl, f0l)
-        inverse_r = right_stat()
+        norm_l = left_stat()
+        first(sl, norm_l, xl, f0l)
+        norm_r = right_stat()
         power(xl, f0l, yl)
-        first(sr, inverse_r, xr, f0r)
+        first(sr, norm_r, xr, f0r)
         power(yl, f0l, xl)
         power(xr, f0r, yr)
         power(xl, f0l, yl)
@@ -247,12 +273,14 @@
 
 def on_device(tokens, cotangent):
     width = tokens.shape[1]
+    half = width // C
     z, y, c = lax.axis_index("z"), lax.axis_index("y"), lax.axis_index("c")
     core_swap = [(0, 1), (1, 0)]
 
-    away = half_product(scalar(1 - c), tokens, cotangent)
-    received = lax.ppermute(away, "c", core_swap)
-    rows = half_product(scalar(c), tokens, cotangent) + received
+    their_cotangent = lax.ppermute(cotangent, "c", core_swap)
+    away = lax.dynamic_slice_in_dim(tokens, (1 - c) * half, half, 1)
+    their_tokens = lax.ppermute(away, "c", core_swap)
+    rows = half_product(scalar(c), tokens, cotangent) + product(their_tokens, their_cotangent)
     for groups in (FIRST, SECOND):
         count = len(groups[0])
         parts = rows.reshape(count, rows.shape[0] // count, width)

time: 148 us -> 147 us (level)
  waiting for transfers between devices: 3.11 us -> 0.39 us
  starting transfers between devices: 21.2 us -> 23.8 us
    ppermute x1 -> x2, waiting for transfers between devices: 2.72 us -> 0.01 us  [the longest x1 0.01 us: on_device(): their_tokens = lax.ppermute(away, 'c', core_swap)]
    ppermute x1 -> x2, starting transfers between devices: 8.79 us -> 10.8 us  [the longest x1 8.91 us: on_device(): their_cotangent = lax.ppermute(cotangent, 'c', core_swap)]
  transfers between devices with their start and end apart: 2 -> 3, of which waited for: 2 -> 1; matrix products, arithmetic and copies ran while one was open for 0% -> 1% of each run, Pallas kernels for 2% -> 2%
where the time goes in v7:
time: 147 us
  blocking collectives  89.5 us (61%)
  Pallas kernels  29.5 us (20%)
  starting transfers between devices  23.8 us (16%)
  local copies, waits for them, and re-layouts  2.73 us (2%)
    all_to_all x2, blocking collectives, on_device(): lax.all_to_all(parts, DP, 0, 0, axis_index_groups=groups)  52.5 us
    all_to_all x2, blocking collectives, on_device(): rows = lax.all_to_all(copies, DP, 0, 0, axis_index_groups=groups)  27.1 us
    pallas_call x1, Pallas kernels, precondition(): pl.pallas_call(body, in_specs=[SMEM] + [VMEM] * 5, out_specs=[VMEM, VMEM]...  25.1 us
    ppermute x1, starting transfers between devices, on_device(): theirs = lax.ppermute(rows, 'c', core_swap)  13 us
    all_to_all x1, blocking collectives, on_device(): lax.all_to_all(square, ('c', 'group'), 0, 0).reshape(C * groups * 8, 128)  9.92 us
    ppermute x1, starting transfers between devices, on_device(): their_cotangent = lax.ppermute(cotangent, 'c', core_swap)  8.91 us
  transfers between devices with their start and end apart: 3, of which 1 were waited for; matrix products, arithmetic and copies ran while one was open for 1% of the time, Pallas kernels for 2%

profile of v7, /device:TPU:1, one launch (start us, length us, event | category | flops | bytes accessed | tf_op | source)
XLA Modules:
  0.0 146.7 jit_solution(3607672873156686199)
XLA Ops:
  0.0 0.0 copy-start
  0.0 8.9 %collective-permute-start.1 = (bf16[768,1024]{1,0:T(8,128)(2,1)}, bf16[768,1024]{1,0:T(8,128)(2,1)S(1)}, u32[]{:S(2)}, u32[]{:S(2)}) collective-permute-start(bf16[768,1024]{1,0:T(8,128)(2,1)} %cotangent_ref.1), channel_id=1, source_target_pairs={{0,8},{8,0},{1,9},{9,1},{2,10},{10,2},{3,11},{11,3},{4,12},{12,4},... | collective-permute-start | bytes 4718600 | tf_op jit(solution)/shard_map/ppermute | solution.py:280
  8.9 1.2 constant_dynamic-slice_fusion
  10.1 1.9 %collective-permute-start = (bf16[768,512]{1,0:T(8,128)(2,1)S(1)}, bf16[768,512]{1,0:T(8,128)(2,1)S(1)}, u32[]{:S(2)}, u32[]{:S(2)}) collective-permute-start(bf16[768,512]{1,0:T(8,128)(2,1)S(1)} %constant_dynamic-slice_fusion), channel_id=1, source_target_pairs={{0,8},{8,0},{1,9},{9,1},{2,10},{10,2},{3,11},{11,3},{4,12},{12,4},... | collective-permute-start | bytes 2359304 | tf_op jit(solution)/shard_map/ppermute | solution.py:282
  12.0 0.0 copy-done
  12.1 0.0 copy-start.1
  12.1 1.4 copy-done.1
  13.5 1.0 half_product.1
  14.5 0.0 collective-permute-done.tokens_ref
  14.5 0.0 collective-permute-done.1.cotangent_ref
  14.5 1.0 product.1
  15.5 0.4 add.11
  15.9 34.4 %all_to_all.25 = f32[4,128,1024]{2,1,0:T(8,128)S(1)} all-to-all(f32[4,128,1024]{2,1,0:T(8,128)S(1)} %bitcast.13), channel_id=1, replica_groups={{0,16,128,144},{32,48,160,176},{80,64,208,192},{112,96,240,224},{384,40..., dimensions={0} | all-to-all | bytes 4194304 | tf_op jit(solution)/shard_map/all_to_all | solution.py:287
  50.3 0.2 reduce_sum.18
  50.5 18.1 %all_to_all.26 = f32[8,16,1024]{2,1,0:T(8,128)S(1)} all-to-all(f32[8,16,1024]{2,1,0:T(8,128)S(1)} %bitcast.14), channel_id=1, replica_groups={{0,32,80,112,384,416,464,496},{16,48,64,96,400,432,448,480},{128,160,20..., dimensions={0} | all-to-all | bytes 1048576 | tf_op jit(solution)/shard_map/all_to_all | solution.py:287
  68.7 10.2 %all_to_all.27 = bf16[8,16,1024]{2,1,0:T(8,128)(2,1)S(1)} all-to-all(bf16[8,16,1024]{2,1,0:T(8,128)(2,1)S(1)} %broadcast_in_dim.7), channel_id=1, replica_groups={{0,32,80,112,384,416,464,496},{16,48,64,96,400,432,448,480},{128,160,20..., dimensions={0} | all-to-all | bytes 524288 | tf_op jit(solution)/shard_map/all_to_all | solution.py:292
  78.9 0.1 broadcast_in_dim.8
  79.0 16.9 %all_to_all.28 = bf16[4,128,1024]{2,1,0:T(8,128)(2,1)S(1)} all-to-all(bf16[4,128,1024]{2,1,0:T(8,128)(2,1)S(1)} %broadcast_in_dim.8), channel_id=1, replica_groups={{0,16,128,144},{32,48,160,176},{80,64,208,192},{112,96,240,224},{384,40..., dimensions={0} | all-to-all | bytes 2097152 | tf_op jit(solution)/shard_map/all_to_all | solution.py:292
  95.9 13.0 %collective-permute-start.2 = (bf16[512,1024]{1,0:T(8,128)(2,1)S(1)}, bf16[512,1024]{1,0:T(8,128)(2,1)S(1)}, u32[]{:S(2)}, u32[]{:S(2)}) collective-permute-start(bf16[512,1024]{1,0:T(8,128)(2,1)S(1)} %bitcast.8), channel_id=1, source_target_pairs={{0,8},{8,0},{1,9},{9,1},{2,10},{10,2},{3,11},{11,3},{4,12},{12,4},... | collective-permute-start | bytes 3145736 | tf_op jit(solution)/shard_map/ppermute | solution.py:294
  108.8 0.1 pad_add_fusion.place_ref
  108.9 1.6 %own_share.1 = (bf16[1024,512]{1,0:T(8,128)(2,1)S(1)}, f32[1024,1024]{1,0:T(8,128)S(1)}, f32[512,512]{1,0:T(8,128)S(1)}) custom-call(bf16[512,1024]{1,0:T(8,128)(2,1)S(1)} %bitcast.9), custom_call_target="tpu_custom_call" | custom-call | flops 2147483648 | bytes 1048576 | tf_op jit(solution)/shard_map/own_share/pallas_call | solution.py:144
  110.5 0.4 collective-permute-done.2.theirs_ref
  110.9 25.1 %precondition.1 = (f32[16,1024]{1,0:T(8,128)S(1)}, f32[128,128]{1,0:T(8,128)S(1)}) custom-call(s32[2]{0:T(128)S(1)} %pad_add_fusion.place_ref, bf16[512,1024]{1,0:T(8,128)(2,1)S(1)} %bitcast.10, bf16[512,1024]{1,0:T(8,128)(2,1)S(1)} %collective-permute-done.2.theirs_ref, bf16[1024,512]{1,0:T(8,128)(2,1)S(1)} %get-tuple-element.10.turned_ref, ...), custom_call_target="tpu_custom_call" | custom-call | flops 24696061952 | bytes 3145728 | tf_op jit(solution)/shard_map/precondition/pallas_call | solution.py:257
  136.1 9.9 %all_to_all.29 = f32[16,8,128]{2,1,0:T(8,128)S(1)} all-to-all(f32[16,8,128]{2,1,0:T(8,128)S(1)} %bitcast.12), channel_id=1, replica_groups=mesh['z'=4,'y'=8,'c'=2,'group'=8] {'c','group'}, dimensions={0} | all-to-all | bytes 131072 | tf_op jit(solution)/shard_map/all_to_all | solution.py:300
  146.0 0.7 normalise.1
  (2 shorter events, 0.0 us)
Async XLA Ops:
  0.0 12.0 %copy-start = (bf16[768,1024]{1,0:T(8,128)(2,1)S(1)}, bf16[768,1024]{1,0:T(8,128)(2,1)}, u32[]{:S(2)}) copy-start(bf16[768,1024]{1,0:T(8,128)(2,1)} %tokens_ref.1) | copy-start | bytes 4718596
  0.0 14.5 %collective-permute-start.1 = (bf16[768,1024]{1,0:T(8,128)(2,1)}, bf16[768,1024]{1,0:T(8,128)(2,1)S(1)}, u32[]{:S(2)}, u32[]{:S(2)}) collective-permute-start(bf16[768,1024]{1,0:T(8,128)(2,1)} %cotangent_ref.1), channel_id=1, source_target_pairs={{0,8},{8,0},{1,9},{9,1},{2,10},{10,2},{3,11},{11,3},{4,12},{12,4},... | collective-permute-start | bytes 4718600 | tf_op jit(solution)/shard_map/ppermute | solution.py:280
  10.1 4.4 %collective-permute-start = (bf16[768,512]{1,0:T(8,128)(2,1)S(1)}, bf16[768,512]{1,0:T(8,128)(2,1)S(1)}, u32[]{:S(2)}, u32[]{:S(2)}) collective-permute-start(bf16[768,512]{1,0:T(8,128)(2,1)S(1)} %constant_dynamic-slice_fusion), channel_id=1, source_target_pairs={{0,8},{8,0},{1,9},{9,1},{2,10},{10,2},{3,11},{11,3},{4,12},{12,4},... | collective-permute-start | bytes 2359304 | tf_op jit(solution)/shard_map/ppermute | solution.py:282
  12.1 1.4 copy-start.1
  95.9 15.1 %collective-permute-start.2 = (bf16[512,1024]{1,0:T(8,128)(2,1)S(1)}, bf16[512,1024]{1,0:T(8,128)(2,1)S(1)}, u32[]{:S(2)}, u32[]{:S(2)}) collective-permute-start(bf16[512,1024]{1,0:T(8,128)(2,1)S(1)} %bitcast.8), channel_id=1, source_target_pairs={{0,8},{8,0},{1,9},{9,1},{2,10},{10,2},{3,11},{11,3},{4,12},{12,4},... | collective-permute-start | bytes 3145736 | tf_op jit(solution)/shard_map/ppermute | solution.py:294
